TPU v7x, 256 devices: a whole 4x4x8 slice. The times are simulated.
256 devices in a mesh: dp: 4 (over y_lo, core), seq: 64 (over x, z, y_hi).
Axes of the slice: x: 4, y: 4 (y_hi: 2, y_lo: 2; y = y_hi * 2 + y_lo), z: 8, core: 2. Of those that a mesh axis runs over, the one named last changes fastest.
Arguments:
- latents: bfloat16 [4, 64, 256, 1152], P('dp', 'seq'), may hold values from -6 to 6
- out_grad: bfloat16 [4, 64, 256, 1152], P('dp', 'seq'), may hold values from -16 to 16
- qkv_spatial: bfloat16 [1728, 1152], replicated, may hold values from -4 to 4
- proj_spatial: bfloat16 [1152, 576], replicated, may hold values from -0.25 to 0.25
- qkv_temporal: bfloat16 [1728, 1152], replicated, may hold values from -4 to 4
- proj_temporal: bfloat16 [1152, 576], replicated, may hold values from -0.25 to 0.25
Outputs:
- latents_grad: bfloat16 [4, 64, 256, 1152], P('dp', 'seq')
- qkv_spatial_grad: float32 [1728, 1152], P('seq', 'dp')
- proj_spatial_grad: float32 [1152, 576], P('seq', 'dp')
- qkv_temporal_grad: float32 [1728, 1152], P('seq', 'dp')
- proj_temporal_grad: float32 [1152, 576], P('seq', 'dp')
All inputs are finite; a program needn't handle non-finite values.
Results may differ from a plain program's by a relative error of at most 0.025.
Values may be sent and summed in bfloat16 or wider, within the bound.
A program may use at most 128 MiB of HBM per device.

v0:
```python
import jax
import jax.numpy as jnp
from jax import lax
from jax.sharding import PartitionSpec as P

HDIM = 72


EPS = 1e-06


def normalize(source):
    widened = source.astype(jnp.float32)
    inverse = lax.rsqrt(jnp.mean(widened * widened, axis=-1, keepdims=True) + EPS)
    return (widened, widened * inverse, inverse)


def split_heads(packed):
    return packed.reshape(packed.shape[:-1] + (packed.shape[-1] // HDIM, HDIM))


def attend(query, keys, values, layout):
    key_layout = layout.replace("l", "m")
    scale = HDIM ** (-0.5)
    scores = (
        jnp.einsum(
            layout + "," + key_layout + "->bhlm",
            split_heads(query),
            split_heads(keys),
            preferred_element_type=jnp.float32,
        )
        * scale
    )
    attn_probs = jax.nn.softmax(scores, axis=-1)
    rounded = attn_probs.astype(jnp.bfloat16)
    attn_out = jnp.einsum(
        "bhlm," + key_layout + "->" + layout,
        rounded,
        split_heads(values),
        preferred_element_type=jnp.float32,
    )
    return (attn_out.astype(jnp.bfloat16).reshape(query.shape), attn_probs, rounded)


def block_forward(source, qkv_weight, out_weight, layout):
    widened, normed, inverse = normalize(source)
    hidden = normed.astype(jnp.bfloat16)
    packed = jnp.einsum(
        "...d,od->...o", hidden, qkv_weight, preferred_element_type=jnp.float32
    ).astype(jnp.bfloat16)
    width = packed.shape[-1] // 3
    query = packed[..., :width]
    keys = packed[..., width : 2 * width]
    values = packed[..., 2 * width :]
    attn_out, attn_probs, rounded = attend(query, keys, values, layout)
    branch = jnp.einsum("...c,dc->...d", attn_out, out_weight, preferred_element_type=jnp.float32)
    result = (widened + branch).astype(jnp.bfloat16)
    return (result, (hidden, normed, inverse, query, keys, values, attn_out, attn_probs, rounded))


def attend_back(d_attn, query, keys, values, attn_out, attn_probs, rounded, layout):
    key_layout = layout.replace("l", "m")
    scale = HDIM ** (-0.5)
    grad_heads = split_heads(d_attn)
    d_probs = jnp.einsum(
        layout + "," + key_layout + "->bhlm",
        grad_heads,
        split_heads(values),
        preferred_element_type=jnp.float32,
    )
    d_values = jnp.einsum(
        "bhlm," + layout + "->" + key_layout,
        rounded,
        grad_heads,
        preferred_element_type=jnp.float32,
    )
    offset = jnp.einsum(
        layout + "," + layout + "->bhl",
        grad_heads,
        split_heads(attn_out),
        preferred_element_type=jnp.float32,
    )
    d_scores = (attn_probs * (d_probs - offset[..., None]) * scale).astype(jnp.bfloat16)
    d_query = jnp.einsum(
        "bhlm," + key_layout + "->" + layout,
        d_scores,
        split_heads(keys),
        preferred_element_type=jnp.float32,
    )
    d_keys = jnp.einsum(
        "bhlm," + layout + "->" + key_layout,
        d_scores,
        split_heads(query),
        preferred_element_type=jnp.float32,
    )
    pieces = [
        d_query.reshape(query.shape),
        d_keys.reshape(query.shape),
        d_values.reshape(query.shape),
    ]
    return jnp.concatenate(pieces, axis=-1).astype(jnp.bfloat16)


def block_backward(d_next, qkv_weight, out_weight, saved, layout):
    hidden, normed, inverse, query, keys, values, attn_out, attn_probs, rounded = saved
    width_d = d_next.shape[-1]
    flat_grad = d_next.reshape(-1, width_d)
    flat_attn = attn_out.reshape(-1, attn_out.shape[-1])
    contract = (((0,), (0,)), ((), ()))
    out_grad_w = lax.dot_general(flat_grad, flat_attn, contract, preferred_element_type=jnp.float32)
    d_attn = jnp.dot(flat_grad, out_weight, preferred_element_type=jnp.float32).astype(jnp.bfloat16)
    d_attn = d_attn.reshape(attn_out.shape)
    d_packed = attend_back(d_attn, query, keys, values, attn_out, attn_probs, rounded, layout)
    flat_packed = d_packed.reshape(-1, d_packed.shape[-1])
    qkv_grad_w = lax.dot_general(
        flat_packed, hidden.reshape(-1, width_d), contract, preferred_element_type=jnp.float32
    )
    d_hidden = jnp.dot(flat_packed, qkv_weight, preferred_element_type=jnp.float32).reshape(
        d_next.shape
    )
    d_source = d_next.astype(jnp.float32) + inverse * (
        d_hidden - normed * jnp.mean(d_hidden * normed, axis=-1, keepdims=True)
    )
    return (d_source.astype(jnp.bfloat16), qkv_grad_w, out_grad_w)


def by_owner(matrix, owners):
    return matrix.reshape((owners, matrix.shape[0] // owners) + matrix.shape[1:])


def reduce_grads(qkv_grad_w, out_grad_w):
    seq_count = lax.axis_size("seq")
    landed = (
        lax.all_to_all(
            by_owner(qkv_grad_w, seq_count).astype(jnp.bfloat16),
            "seq",
            split_axis=0,
            concat_axis=0,
            tiled=True,
        ).astype(jnp.float32),
        lax.all_to_all(
            by_owner(out_grad_w, seq_count).astype(jnp.bfloat16),
            "seq",
            split_axis=0,
            concat_axis=0,
            tiled=True,
        ).astype(jnp.float32),
    )
    shares = (jnp.sum(landed[0], axis=0), jnp.sum(landed[1], axis=0))
    return (
        lax.psum_scatter(
            shares[0].astype(jnp.bfloat16), "dp", scatter_dimension=1, tiled=True
        ).astype(jnp.float32),
        lax.psum_scatter(
            shares[1].astype(jnp.bfloat16), "dp", scatter_dimension=1, tiled=True
        ).astype(jnp.float32),
    )


def per_device(latents, out_grad, qkv_spatial, proj_spatial, qkv_temporal, proj_temporal):
    source = latents[0]
    upstream = out_grad[0]
    residual, saved_space = block_forward(source, qkv_spatial, proj_spatial, "blhd")
    residual_time, upstream_time = (
        lax.all_to_all(residual, "seq", split_axis=1, concat_axis=0, tiled=True),
        lax.all_to_all(upstream, "seq", split_axis=1, concat_axis=0, tiled=True),
    )
    unused, saved_time = block_forward(residual_time, qkv_temporal, proj_temporal, "lbhd")
    d_residual_time, qkv_time, out_time = block_backward(
        upstream_time, qkv_temporal, proj_temporal, saved_time, "lbhd"
    )
    time_sums = reduce_grads(qkv_time, out_time)
    d_residual = lax.all_to_all(d_residual_time, "seq", split_axis=0, concat_axis=1, tiled=True)
    d_source, qkv_space, out_space = block_backward(
        d_residual, qkv_spatial, proj_spatial, saved_space, "blhd"
    )
    space_sums = reduce_grads(qkv_space, out_space)
    return (d_source[None], space_sums[0], space_sums[1], time_sums[0], time_sums[1])


def solution(mesh):
    placed = (P("dp", "seq", None, None), P("dp", "seq", None, None), P(), P(), P(), P())
    return jax.shard_map(
        per_device,
        mesh=mesh,
        in_specs=placed,
        out_specs=(
            P("dp", "seq", None, None),
            P("seq", "dp"),
            P("seq", "dp"),
            P("seq", "dp"),
            P("seq", "dp"),
        ),
        check_vma=False,
    )
```

profile of v0, /device:TPU:1, one launch (start us, length us, event | category | flops | bytes accessed | tf_op | source)
XLA Modules:
  0.0 554.2 jit_solution(5756780180264454345)
XLA Ops:
  9.1 3.7 fusion.11
  20.6 5.0 reduce.20
  25.6 2.6 reshape.377
  28.2 15.6 %all-to-all-start.1 = ((bf16[64,2,2304]{2,1,0:T(2,128)(2,1)}), bf16[64,2,2304]{2,1,0:T(2,128)(2,1)}, u32[]{:S(2)}, u32[]{:S(2)}) async-start(bf16[64,2,2304]{2,1,0:T(2,128)(2,1)} %reshape.377), calls=%async_computation.1 | async-start | bytes 1179648 | tf_op jit(solution)/shard_map/all_to_all | solution.py:165
  45.7 5.0 reduce.19
  50.8 2.6 reshape.375
  53.4 8.8 %all-to-all-done.1 = bf16[64,2,2304]{2,1,0:T(2,128)(2,1)} async-done(((bf16[64,2,2304]{2,1,0:T(2,128)(2,1)}), bf16[64,2,2304]{2,1,0:T(2,128)(2,1)}, u32[]{:S(2)}, u32[]{:S(2)}) %all-to-all-start.1) | async-done | bytes 589856 | tf_op jit(solution)/shard_map/all_to_all | solution.py:165
  62.2 7.7 %all-to-all-start = ((bf16[64,2,2304]{2,1,0:T(2,128)(2,1)}), bf16[64,2,2304]{2,1,0:T(2,128)(2,1)}, u32[]{:S(2)}, u32[]{:S(2)}) async-start(bf16[64,2,2304]{2,1,0:T(2,128)(2,1)} %reshape.375), calls=%async_computation | async-start | bytes 1179648 | tf_op jit(solution)/shard_map/all_to_all | solution.py:166
  70.0 3.8 reshape.378
  75.1 12.9 %all-to-all-done = bf16[64,2,2304]{2,1,0:T(2,128)(2,1)} async-done(((bf16[64,2,2304]{2,1,0:T(2,128)(2,1)}), bf16[64,2,2304]{2,1,0:T(2,128)(2,1)}, u32[]{:S(2)}, u32[]{:S(2)}) %all-to-all-start) | async-done | bytes 589856 | tf_op jit(solution)/shard_map/all_to_all | solution.py:166
  88.0 4.7 reshape.376
  92.7 5.8 %convert_reduce_fusion = f32[256,1152]{1,0:T(8,128)} fusion(bf16[256,1,1152]{2,1,0:T(2,128)(2,1)} %reshape.376), kind=kLoop, calls=%fused_computation.59 | loop fusion | flops 294912 | bytes 1769472 | tf_op jit(solution)/shard_map/convert_element_type | solution.py:121
  98.4 2.6 convolution_convert_fusion.10
  102.9 2.3 reshape_reshape.8
  105.2 2.3 bitcast_convert_fusion
  107.7 3.0 reshape.354
  110.7 4.0 fusion.8
  115.7 2.4 reshape.347
  118.1 2.3 reshape.349
  120.4 2.3 reshape.346
  122.7 2.7 fusion.87
  125.4 2.7 fusion.25
  133.2 2.6 reshape.352
  151.2 4.4 multiply_reduce_fusion.1
  157.2 8.1 %all-to-all-start.2 = ((bf16[64,4,1152]{2,1,0:T(4,128)(2,1)}), bf16[64,4,1152]{2,1,0:T(4,128)(2,1)}, u32[]{:S(2)}, u32[]{:S(2)}) async-start(bf16[64,4,1152]{2,1,0:T(4,128)(2,1)} %copy.123), calls=%async_computation.2 | async-start | bytes 1179648 | tf_op jit(solution)/shard_map/all_to_all | solution.py:173
  169.7 3.0 fusion.6
  172.7 2.6 copy.140
  175.3 3.8 convert_element_type.245
  179.1 3.7 all-to-all-done.2
  182.8 8.8 %all-to-all-start.6 = ((bf16[64,18,576]{2,1,0:T(8,128)(2,1)}), bf16[64,18,576]{2,1,0:T(8,128)(2,1)}, u32[]{:S(2)}, u32[]{:S(2)}) async-start(bf16[64,18,576]{2,1,0:T(8,128)(2,1)} %convert_element_type.245), calls=%async_computation.6 | async-start | bytes 3932160 | tf_op jit(solution)/shard_map/all_to_all | solution.py:141
  202.0 36.7 %all-to-all-done.6 = bf16[64,18,576]{2,1,0:T(8,128)(2,1)} async-done(((bf16[64,18,576]{2,1,0:T(8,128)(2,1)}), bf16[64,18,576]{2,1,0:T(8,128)(2,1)}, u32[]{:S(2)}, u32[]{:S(2)}) %all-to-all-start.6) | async-done | bytes 1327136 | tf_op jit(solution)/shard_map/all_to_all | solution.py:141
  238.7 8.2 %all-to-all-start.4 = ((bf16[64,18,576]{2,1,0:T(8,128)(2,1)}), bf16[64,18,576]{2,1,0:T(8,128)(2,1)}, u32[]{:S(2)}, u32[]{:S(2)}) async-start(bf16[64,18,576]{2,1,0:T(8,128)(2,1)} %copy.132), calls=%async_computation.4 | async-start | bytes 3932160 | tf_op jit(solution)/shard_map/all_to_all | solution.py:141
  247.0 2.2 copy.133
  260.3 2.3 copy.136
  264.8 3.4 convolution_convert_fusion
  268.2 4.5 copy.138
  272.7 21.6 %all-to-all-done.4 = bf16[64,18,576]{2,1,0:T(8,128)(2,1)} async-done(((bf16[64,18,576]{2,1,0:T(8,128)(2,1)}), bf16[64,18,576]{2,1,0:T(8,128)(2,1)}, u32[]{:S(2)}, u32[]{:S(2)}) %all-to-all-start.4) | async-done | bytes 1327136 | tf_op jit(solution)/shard_map/all_to_all | solution.py:141
  294.3 8.2 %all-to-all-start.5 = ((bf16[64,27,1152]{2,1,0:T(8,128)(2,1)}), bf16[64,27,1152]{2,1,0:T(8,128)(2,1)}, u32[]{:S(2)}, u32[]{:S(2)}) async-start(bf16[64,27,1152]{2,1,0:T(8,128)(2,1)} %copy.138), calls=%async_computation.5 | async-start | bytes 9437184 | tf_op jit(solution)/shard_map/all_to_all | solution.py:134
  310.2 2.8 convolution_convert_fusion.1
  313.0 4.4 copy.129
  317.5 91.5 %all-to-all-done.5 = bf16[64,27,1152]{2,1,0:T(8,128)(2,1)} async-done(((bf16[64,27,1152]{2,1,0:T(8,128)(2,1)}), bf16[64,27,1152]{2,1,0:T(8,128)(2,1)}, u32[]{:S(2)}, u32[]{:S(2)}) %all-to-all-start.5) | async-done | bytes 3981344 | tf_op jit(solution)/shard_map/all_to_all | solution.py:134
  409.0 8.3 %all-to-all-start.3 = ((bf16[64,27,1152]{2,1,0:T(8,128)(2,1)}), bf16[64,27,1152]{2,1,0:T(8,128)(2,1)}, u32[]{:S(2)}, u32[]{:S(2)}) async-start(bf16[64,27,1152]{2,1,0:T(8,128)(2,1)} %copy.129), calls=%async_computation.3 | async-start | bytes 9437184 | tf_op jit(solution)/shard_map/all_to_all | solution.py:134
  423.0 4.6 fusion.26
  427.5 3.1 reduce_sum.110
  431.6 91.9 %all-to-all-done.3 = bf16[64,27,1152]{2,1,0:T(8,128)(2,1)} async-done(((bf16[64,27,1152]{2,1,0:T(8,128)(2,1)}), bf16[64,27,1152]{2,1,0:T(8,128)(2,1)}, u32[]{:S(2)}, u32[]{:S(2)}) %all-to-all-start.3) | async-done | bytes 3981344 | tf_op jit(solution)/shard_map/all_to_all | solution.py:134
  523.5 3.1 reduce_sum.108
  527.5 2.4 fusion.45
  534.5 11.1 %reduce-scatter.13.cloned.1.call-done = bf16[288,27]{1,0:T(8,128)(2,1)} async-done(((bf16[1152,27]{1,0:T(8,128)(2,1)}), bf16[288,27]{1,0:T(8,128)(2,1)}) %reduce-scatter.13.cloned.1.call-update) | async-done | bytes 15568
  (141 shorter events, 87.4 us)
Async XLA Ops:
  7.2 11.1 %copy-start = (bf16[1152,576]{0,1:T(8,128)(2,1)S(1)}, bf16[1152,576]{0,1:T(8,128)(2,1)}, u32[]{:S(2)}) copy-start(bf16[1152,576]{0,1:T(8,128)(2,1)} %param.9) | copy-start | bytes 3981316
  8.6 0.6 copy-start.28
  12.9 2.3 copy-start.14
  12.9 2.2 copy-start.16
  13.0 4.0 copy-start.18
  17.0 1.0 copy-start.2
  17.0 1.4 copy-start.1
  28.2 34.0 %all-to-all-start.1 = ((bf16[64,2,2304]{2,1,0:T(2,128)(2,1)}), bf16[64,2,2304]{2,1,0:T(2,128)(2,1)}, u32[]{:S(2)}, u32[]{:S(2)}) async-start(bf16[64,2,2304]{2,1,0:T(2,128)(2,1)} %reshape.377), calls=%async_computation.1 | async-start | bytes 1179648 | tf_op jit(solution)/shard_map/all_to_all | solution.py:165
  62.2 25.8 %all-to-all-start = ((bf16[64,2,2304]{2,1,0:T(2,128)(2,1)}), bf16[64,2,2304]{2,1,0:T(2,128)(2,1)}, u32[]{:S(2)}, u32[]{:S(2)}) async-start(bf16[64,2,2304]{2,1,0:T(2,128)(2,1)} %reshape.375), calls=%async_computation | async-start | bytes 1179648 | tf_op jit(solution)/shard_map/all_to_all | solution.py:166
  92.7 5.8 %copy-start.4 = (bf16[256,1,1152]{2,1,0:T(2,128)(2,1)S(1)}, bf16[256,1,1152]{2,1,0:T(2,128)(2,1)}, u32[]{:S(2)}) copy-start(bf16[256,1,1152]{2,1,0:T(2,128)(2,1)} %reshape.376) | copy-start | bytes 1769476
  125.4 2.7 copy-start.26
  125.4 2.7 copy-start.27
  125.4 2.7 copy-start.30
  128.1 1.7 copy-start.10
  129.8 1.0 copy-start.11
  130.9 1.2 copy-start.12
  151.2 4.4 copy-start.6
  151.2 4.4 copy-start.7
  157.2 25.7 %all-to-all-start.2 = ((bf16[64,4,1152]{2,1,0:T(4,128)(2,1)}), bf16[64,4,1152]{2,1,0:T(4,128)(2,1)}, u32[]{:S(2)}, u32[]{:S(2)}) async-start(bf16[64,4,1152]{2,1,0:T(4,128)(2,1)} %copy.123), calls=%async_computation.2 | async-start | bytes 1179648 | tf_op jit(solution)/shard_map/all_to_all | solution.py:173
  182.8 55.9 %all-to-all-start.6 = ((bf16[64,18,576]{2,1,0:T(8,128)(2,1)}), bf16[64,18,576]{2,1,0:T(8,128)(2,1)}, u32[]{:S(2)}, u32[]{:S(2)}) async-start(bf16[64,18,576]{2,1,0:T(8,128)(2,1)} %convert_element_type.245), calls=%async_computation.6 | async-start | bytes 3932160 | tf_op jit(solution)/shard_map/all_to_all | solution.py:141
  238.7 55.6 %all-to-all-start.4 = ((bf16[64,18,576]{2,1,0:T(8,128)(2,1)}), bf16[64,18,576]{2,1,0:T(8,128)(2,1)}, u32[]{:S(2)}, u32[]{:S(2)}) async-start(bf16[64,18,576]{2,1,0:T(8,128)(2,1)} %copy.132), calls=%async_computation.4 | async-start | bytes 3932160 | tf_op jit(solution)/shard_map/all_to_all | solution.py:141
  246.9 2.3 copy-start.8
  246.9 3.4 copy-start.13
  272.7 29.8 %copy-start.5 = (bf16[256,1152]{1,0:T(8,128)(2,1)S(1)}, bf16[256,1152]{1,0:T(8,128)(2,1)}, u32[]{:S(2)}) copy-start(bf16[256,1152]{1,0:T(8,128)(2,1)} %all_to_all.38) | copy-start | bytes 1769476
  294.3 114.7 %all-to-all-start.5 = ((bf16[64,27,1152]{2,1,0:T(8,128)(2,1)}), bf16[64,27,1152]{2,1,0:T(8,128)(2,1)}, u32[]{:S(2)}, u32[]{:S(2)}) async-start(bf16[64,27,1152]{2,1,0:T(8,128)(2,1)} %copy.138), calls=%async_computation.5 | async-start | bytes 9437184 | tf_op jit(solution)/shard_map/all_to_all | solution.py:134
  302.5 1.2 copy-start.3
  302.5 1.7 copy-start.19
  303.1 1.7 copy-start.9
  304.8 2.4 copy-start.20
  304.8 1.1 copy-start.17
  305.9 1.0 copy-start.15
  306.8 0.7 copy-start.22
  307.1 0.7 copy-start.24
  409.0 114.5 %all-to-all-start.3 = ((bf16[64,27,1152]{2,1,0:T(8,128)(2,1)}), bf16[64,27,1152]{2,1,0:T(8,128)(2,1)}, u32[]{:S(2)}, u32[]{:S(2)}) async-start(bf16[64,27,1152]{2,1,0:T(8,128)(2,1)} %copy.129), calls=%async_computation.3 | async-start | bytes 9437184 | tf_op jit(solution)/shard_map/all_to_all | solution.py:134
  417.3 112.7 %reduce-scatter.19.cloned.1.call-start = ((), (), s32[]{:S(2)}) async-start(), calls=%async_computation.14 | async-start | bytes 184320
  419.3 3.7 copy-start.21
  419.3 3.7 copy-start.23
  419.3 3.7 copy-start.25
  419.3 3.7 copy-start.29
  420.1 111.3 %reduce-scatter.15.cloned.1.call-start = ((), (), s32[]{:S(2)}) async-start(), calls=%async_computation.12 | async-start | bytes 184320
  422.9 110.0 %reduce-scatter.17.cloned.1.call-start = ((), (), s32[]{:S(2)}) async-start(), calls=%async_computation.13 | async-start | bytes 368640
  431.6 114.1 %reduce-scatter.13.cloned.1.call-start = ((), (), s32[]{:S(2)}) async-start(), calls=%async_computation.11 | async-start | bytes 368640
Sparse Core Ops, SparseCore 0:
  420.6 23.4 reduce-scatter.18
  446.8 20.2 reduce-scatter.14
  469.6 23.7 reduce-scatter.16
  527.6 17.9 reduce-scatter.12
where the time goes:
time: 564 us; the launch traced here: 554 us
  waiting for transfers between devices  278 us (49%)
  local copies, waits for them, and re-layouts  112 us (20%)
  starting transfers between devices  65 us (12%)
  matrix products  45.7 us (8%)
  other arithmetic  38.9 us (7%)
  between operations  14.7 us (3%)
    all_to_all x2, waiting for transfers between devices, reduce_grads(): lax.all_to_all(by_owner(qkv_grad_w, seq_count).astype(jnp.bfloat16), 'seq...  183 us
    all_to_all x2, waiting for transfers between devices, reduce_grads(): lax.all_to_all(by_owner(out_grad_w, seq_count).astype(jnp.bfloat16), 'seq...  58.3 us
    unnamed x75, local copies, waits for them, and re-layouts  26.5 us
    concatenate x8, local copies, waits for them, and re-layouts, attend_back(): return jnp.concatenate(pieces, axis=-1).astype(jnp.bfloat16)  17.7 us
    all_to_all x2, starting transfers between devices, reduce_grads(): lax.all_to_all(by_owner(out_grad_w, seq_count).astype(jnp.bfloat16), 'seq...  17 us
    all_to_all x2, starting transfers between devices, reduce_grads(): lax.all_to_all(by_owner(qkv_grad_w, seq_count).astype(jnp.bfloat16), 'seq...  16.5 us
    all_to_all x1, starting transfers between devices, per_device(): lax.all_to_all(residual, 'seq', split_axis=1, concat_axis=0, tiled=True)  15.6 us
    all_to_all x1, waiting for transfers between devices, per_device(): lax.all_to_all(upstream, 'seq', split_axis=1, concat_axis=0, tiled=True)  12.9 us
  transfers between devices with their start and end apart: 11, of which 8 were waited for; matrix products, arithmetic and copies ran while one was open for 18% of the time, Pallas kernels for 0%

commit v1 on v0

v1 whole, which is shorter than its diff:
```python
import jax
import jax.numpy as jnp
from jax import lax
from jax.experimental import pallas as pl
from jax.experimental.pallas import tpu as pltpu
from jax.sharding import PartitionSpec as P

HDIM = 72
HEADS = 8
HD = HDIM * HEADS
PAD = 640
D = 1152
TOK = 256
GROUPS = 64
OWN = TOK // GROUPS
EPS = 1e-06
SCALE = HDIM ** (-0.5)
NEG = -1e30
MESH = pl.DeviceIdType.MESH
VMEM = pltpu.VMEM
F32 = jnp.float32
BF16 = jnp.bfloat16
LIMIT = 60 * 2**20

QROWS = 288
PROWS = 96
ROWS = QROWS + PROWS
PART = ROWS // 2
TILES = 16
QWIN = 384
PWIN = 256


def dot(a, b, dims=((1,), (0,))):
    return lax.dot_general(a, b, (dims, ((), ())), preferred_element_type=F32)


NT = ((1,), (1,))
TN = ((0,), (0,))


def window(head):
    low = head * HDIM // 128 * 128
    return low, -(-(head + 1) * HDIM // 128) * 128


def head_mask(head, low, high):
    lane = lax.broadcasted_iota(jnp.int32, (1, high - low), 1) + low
    return ((lane >= head * HDIM) & (lane < (head + 1) * HDIM)).astype(F32).astype(BF16)


def normalize(x):
    inverse = lax.rsqrt(jnp.mean(x * x, axis=-1, keepdims=True) + EPS)
    return x * inverse, inverse


def project(hidden, w_ref, targets):
    for i, target in enumerate(targets):
        target[:, :HD] = dot(hidden, w_ref[i * HD : (i + 1) * HD, :], NT).astype(BF16)
        target[:, HD:] = jnp.zeros((TOK, PAD - HD), BF16)


def softmax(qm, k, keep):
    s = dot(qm, k, NT) * SCALE
    if keep is not None:
        s = jnp.where(keep, s, NEG)
    e = jnp.exp(s - jnp.max(s, axis=-1, keepdims=True))
    return e * (1.0 / jnp.sum(e, axis=-1, keepdims=True))


def same_position():
    rows = lax.broadcasted_iota(jnp.int32, (TOK, TOK), 0)
    columns = lax.broadcasted_iota(jnp.int32, (TOK, TOK), 1)
    return lax.rem(rows, OWN) == lax.rem(columns, OWN)


def attention(q, k, v, acc, attn, keep):
    acc[...] = jnp.zeros_like(acc)
    for h in range(HEADS):
        low, high = window(h)
        mask = head_mask(h, low, high)
        probs = softmax(q[:, low:high] * mask, k[:, low:high], keep)
        acc[:, low:high] += dot(probs.astype(BF16), v[:, low:high] * mask)
    attn[...] = acc[...].astype(BF16)


def attention_back(q, k, v, attn, da, accs, keep, hooks):
    for acc in accs:
        acc[...] = jnp.zeros_like(acc)
    dq, dk, dv = accs
    for h in range(HEADS):
        if h in hooks:
            hooks[h]()
        low, high = window(h)
        mask = head_mask(h, low, high)
        qm = q[:, low:high] * mask
        km = k[:, low:high] * mask
        dam = da[:, low:high] * mask
        probs = softmax(qm, k[:, low:high], keep)
        d_probs = dot(dam, v[:, low:high], NT)
        dv[:, low:high] += dot(probs.astype(BF16), dam, TN)
        offset = jnp.sum(dam.astype(F32) * attn[:, low:high].astype(F32), axis=-1, keepdims=True)
        ds = (probs * (d_probs - offset) * SCALE).astype(BF16)
        dq[:, low:high] += dot(ds, km)
        dk[:, low:high] += dot(ds, qm, TN)


def pack(accs, dpk):
    for i, acc in enumerate(accs):
        dpk[:, i * PAD : (i + 1) * PAD] = acc[...].astype(BF16)


def block_back(dy, x, w_ref, dpk):
    d_hidden = jnp.zeros((TOK, D), F32)
    for i in range(3):
        part = dpk[:, i * PAD : i * PAD + HD]
        d_hidden = d_hidden + dot(part, w_ref[i * HD : (i + 1) * HD, :])
    normed, inverse = normalize(x)
    along = jnp.mean(d_hidden * normed, axis=-1, keepdims=True)
    return dy.astype(F32) + inverse * (d_hidden - normed * along)


def to_blocks(value, ref):
    for t in range(D // 128):
        ref[:, t, :, :] = value[:, t * 128 : (t + 1) * 128].reshape(GROUPS, OWN, 128)


def from_blocks(ref):
    return jnp.concatenate([ref[:, t, :, :].reshape(TOK, 128) for t in range(D // 128)], axis=1)


def at_xyz(x, y, z, core):
    return lax.rem(y, 2) * 2 + core, (x * 8 + z) * 2 + lax.div(y, 2)


def lane_shards(tile):
    x, y_hi, z_hi = tile // 4, tile // 2 % 2, tile % 2
    return [(x * 8 + z_hi * 4 + i) * 2 + y_hi for i in range(4)]


def qplace(column):
    return column + (PAD - HD) * (column // HD)


def qlow(tile):
    return min(qplace(27 * lane_shards(tile)[0]) // 128 * 128, 3 * PAD - QWIN)


def plow(tile):
    return min(18 * lane_shards(tile)[0] // 128 * 128, D - PWIN)


def choice(low, window, lead, first, count, step, edges):
    row = lax.broadcasted_iota(jnp.int32, (window, 128), 0) + low
    lane = lax.broadcasted_iota(jnp.int32, (1, 128), 1)
    inner = (lane & 31) - first
    wanted = lead + lax.shift_right_logical(lane, 5) * step + inner
    gaps = sum((jnp.where(wanted >= e, PAD - HD, 0) for e in edges), jnp.zeros_like(wanted))
    wanted = jnp.where((inner >= 0) & (inner < count), wanted + gaps, -1)
    return (row == wanted).astype(F32).astype(BF16)


def spreaders(qs, ps):
    for tile in range(TILES):
        shard = lane_shards(tile)[0]
        qs[tile] = choice(qlow(tile), QWIN, 27 * shard, 0, 27, 54, (HD, 2 * HD))
        low = plow(tile)
        ps[tile, :, 0:128] = choice(low, PWIN, 18 * shard, 0, 18, 36, ())
        ps[tile, :, 128:256] = choice(low, PWIN, 18 * shard, 18, 9, 36, ())
        ps[tile, :, 256:384] = choice(low, PWIN, 18 * shard + 9, 18, 9, 36, ())


def gradients(qs, ps, hcat, a01, a2, dpk, dy, mq, mp, ga, gb):
    for x in range(4):
        for t in range(4):
            tile, here = x * 4 + t, slice(t * 128, (t + 1) * 128)
            low = qlow(tile)
            mq[:, here] = dot(dpk[:, low : low + QWIN], qs[tile]).astype(BF16)
            low = plow(tile)
            spread = dot(dy[:, low : low + PWIN], ps[tile]).astype(BF16)
            for j in range(3):
                mp[j, :, here] = spread[:, j * 128 : (j + 1) * 128]
        qkv = dot(hcat[...], mq[...])
        proj = dot(a01[...], mp[0])
        last = [dot(a2[...], mp[1]), dot(a2[...], mp[2])]
        for y_lo in range(2):
            for y_hi in range(2):
                here = slice(y_hi * 256, (y_hi + 1) * 256)
                row = y_lo * QROWS
                ga[x, y_hi, y_lo] = qkv[row : row + PART, here].astype(BF16)
                gb[x, y_hi, y_lo, 0:96] = qkv[row + PART : row + QROWS, here].astype(BF16)
                for g in range(2):
                    both = proj[y_lo * 96 + g * 48 : y_lo * 96 + g * 48 + 48, here]
                    both = both + last[g][y_lo * 48 : y_lo * 48 + 48, here]
                    gb[x, y_hi, y_lo, 96 + 48 * g : 144 + 48 * g] = both.astype(BF16)


class Ring:
    def __init__(self, copy, block, relay, near, place, along):
        self.copy, self.block, self.relay, self.near = copy, block, relay, near
        self.up, self.down = lax.rem(place + 1, 4), lax.rem(place + 3, 4)
        self.two = lax.rem(place + 2, 4)
        self.to_up, self.to_down = along(1), along(3)

    def first(self):
        copy, block, near = self.copy, self.block, self.near
        self.on_way = (
            copy(block(self.two, 0), self.relay.at[0], self.to_up),
            copy(block(self.two, 1), self.relay.at[1], self.to_down),
        )
        self.copies = [
            copy(block(self.up, 1), near.at[0, 1], self.to_up),
            copy(block(self.down, 0), near.at[1, 0], self.to_down),
        ]

    def second(self):
        copy, block, near = self.copy, self.block, self.near
        steps = ((self.up, 0, self.to_up), (self.down, 1, self.to_down))
        for side, (place, half, to) in enumerate(steps):
            self.on_way[side].wait()
            ref = block(place, half)
            ref[...] = (ref[...].astype(F32) + self.relay[side].astype(F32)).astype(BF16)
            self.copies.append(copy(ref, near.at[side, half], to))

    def total(self, own):
        for c in self.copies:
            c.wait()
        near = self.near[0].astype(F32) + self.near[1].astype(F32)
        return own.astype(F32) + near.reshape(own.shape)


def kernel(
    x_in, dy_in, ws_in, ps_in, wt_in, pt_in,
    dx_out, gqs, gps, gqt, gpt,
    x_v, dy_v, ws, ps, wt, pt,
    dyb, dyr, nxb, nxr, dxb, dxr,
    qs, ks, vs, os, qt, kt, vt, ot, da, acc0, acc1, acc2,
    ht, at, hcat, a01, a2, dpk, dyf,
    spread_q, spread_p, mq, mp,
    ga, gb, relay_a, relay_b, near_a, near_b,
    ha, hb, relay2_a, relay2_b, near2_a, near2_b,
    zs, zr,
    send, recv, all_send, all_recv, local,
):
    dp, me = lax.axis_index("dp"), lax.axis_index("seq")
    core, y_lo = lax.rem(dp, 2), lax.div(dp, 2)
    y_hi, z, x = lax.rem(me, 2), lax.rem(lax.div(me, 2), 8), lax.div(me, 16)
    y = y_hi * 2 + y_lo
    n = GROUPS
    pair = at_xyz(x, y, z, 1 - core)

    def along_x(k):
        return at_xyz(lax.rem(x + k, 4), y, z, core)

    def along_y(k):
        return at_xyz(x, lax.rem(y + k, 4), z, core)

    def along_z(k):
        return at_xyz(x, y, lax.rem(z + k, 8), core)

    counts = [0, 0]

    def here(source, target):
        c = pltpu.make_async_copy(source, target, local.at[counts[0]])
        counts[0] += 1
        c.start()
        return c

    def copy(source, target, to):
        i = counts[1]
        counts[1] += 1
        c = pltpu.make_async_remote_copy(
            src_ref=source,
            dst_ref=target,
            send_sem=send.at[i],
            recv_sem=recv.at[i],
            device_id=to,
            device_id_type=MESH,
        )
        c.start()
        return c

    get_dy = here(dy_in, dy_v)
    get_x = here(x_in, x_v)
    get_ws = here(ws_in, ws)
    get_ps = here(ps_in, ps)
    get_wt = here(wt_in, wt)
    get_pt = here(pt_in, pt)

    barrier = pltpu.get_barrier_semaphore()

    @pl.loop(1, n)
    def _(i):
        pl.semaphore_signal(barrier, inc=1, device_id=(dp, lax.rem(me + i, n)), device_id_type=MESH)

    for friend in (pair, along_y(1), along_y(3)):
        pl.semaphore_signal(barrier, inc=1, device_id=friend, device_id_type=MESH)

    def exchange_start(j, source, target):
        @pl.loop(1, n)
        def _(i):
            to = lax.rem(me + i, n)
            pltpu.make_async_remote_copy(
                src_ref=source.at[to],
                dst_ref=target.at[me],
                send_sem=all_send.at[j],
                recv_sem=all_recv.at[j],
                device_id=(dp, to),
                device_id_type=MESH,
            ).start()

        return here(source.at[me], target.at[me])

    def exchange_wait(j, source, target, own):
        own.wait()
        pltpu.make_async_remote_copy(
            src_ref=source.at[pl.ds(0, n - 1)],
            dst_ref=target.at[pl.ds(0, n - 1)],
            send_sem=all_send.at[j],
            recv_sem=all_recv.at[j],
            device_id=pair,
            device_id_type=MESH,
        ).wait()

    far = pl.ds(TOK, TOK)

    def share_forward(b):
        copies = []
        for i in range(2):
            block = i * 2 + 1 - core
            rows = pl.ds(pl.multiple_of(block * QROWS, 32), QROWS)
            copies.append(copy(ht.at[b, rows], hcat.at[b, pl.ds(i * QROWS, QROWS), far], pair))
            rows = pl.ds(pl.multiple_of(block * 144, 16), 96)
            copies.append(copy(at.at[b, rows], a01.at[b, pl.ds(i * 96, 96), far], pair))
            rows = pl.ds(pl.multiple_of(block * 144 + 96, 16), 48)
            copies.append(copy(at.at[b, rows], a2.at[b, pl.ds(i * 48, 48), far], pair))
            block = i * 2 + core
            rows = pl.ds(pl.multiple_of(block * QROWS, 32), QROWS)
            hcat[b, i * QROWS : (i + 1) * QROWS, :TOK] = ht[b, rows, :]
            rows = pl.ds(pl.multiple_of(block * 144, 16), 96)
            a01[b, i * 96 : (i + 1) * 96, :TOK] = at[b, rows, :]
            rows = pl.ds(pl.multiple_of(block * 144 + 96, 16), 48)
            a2[b, i * 48 : (i + 1) * 48, :TOK] = at[b, rows, :]
        return copies

    def share(ref, b):
        return copy(ref.at[b, pl.ds(0, TOK)], ref.at[b, far], pair)

    def rings(b):
        first = (
            Ring(copy, lambda i, h: ga.at[b, i, h], relay_a.at[b], near_a.at[b], x, along_x),
            Ring(
                copy,
                lambda i, h: gb.at[b, pl.ds(2 * h, 2), lax.div(i, 2), lax.rem(i, 2)],
                relay_b.at[b], near_b.at[b], y, along_y,
            ),
        )
        half = PART // 2
        second = (
            Ring(copy, lambda i, h: ha.at[b, i, pl.ds(h * half, half)], relay2_a.at[b], near2_a.at[b], y, along_y),
            Ring(copy, lambda i, h: hb.at[b, i, pl.ds(h * half, half)], relay2_b.at[b], near2_b.at[b], x, along_x),
        )
        return first, second

    def weight_terms(b, copies):
        for c in copies:
            c.wait()
        gradients(
            spread_q, spread_p, hcat.at[b], a01.at[b], a2.at[b], dpk.at[b], dyf.at[b], mq, mp, ga.at[b], gb.at[b]
        )

    def between(b, first, second):
        ha[b] = first[0].total(ga[b, x].reshape(4, PART, 256)).astype(BF16)
        second[0].first()
        hb[b] = first[1].total(gb[b, :, y_hi, y_lo]).astype(BF16)
        second[1].first()

    def last(b, second):
        sums = [second[0].total(ha[b, y]), second[1].total(hb[b, x])]
        sums = jnp.concatenate(sums, axis=0).T
        zs[b] = sums.reshape(8, 32, ROWS).astype(BF16)
        copies = []
        for k in range(1, 8):
            copies.append(copy(zs.at[b, lax.rem(z + k, 8)], zr.at[b, k], along_z(k)))
        return copies

    def finish(b, copies, qkv, proj):
        acc = zs[b, z].astype(F32)
        for k in range(1, 8):
            copies[k - 1].wait()
            acc = acc + zr[b, k].astype(F32)
        qkv[...] = acc[:27, :QROWS]
        proj[:, 0:96] = acc[:18, QROWS:]
        proj[0:9, 96:144] = acc[18:27, QROWS : QROWS + 48]
        proj[9:18, 96:144] = acc[18:27, QROWS + 48 :]

    SPACE, TIME = 0, 1

    get_dy.wait()
    to_blocks(dy_v[...], dyb)
    pl.semaphore_wait(barrier, n + 2)
    own_dy = exchange_start(0, dyb, dyr)
    get_x.wait()
    source = x_v[...].astype(F32)
    normed, _ = normalize(source)
    hidden = normed.astype(BF16)
    get_ws.wait()
    project(hidden, ws, (qs, ks, vs))
    attention(qs, ks, vs, acc0, os, None)
    get_ps.wait()
    to_blocks((source + dot(os[:, :HD], ps[...])).astype(BF16), nxb)
    own_next = exchange_start(1, nxb, nxr)
    ht[SPACE] = hidden.T
    at[SPACE] = os[...].T
    shared_s = share_forward(SPACE)
    spreaders(spread_q, spread_p)

    get_wt.wait()
    get_pt.wait()
    exchange_wait(1, nxb, nxr, own_next)
    middle = from_blocks(nxr)
    normed, _ = normalize(middle.astype(F32))
    hidden = normed.astype(BF16)
    ht[TIME] = hidden.T
    project(hidden, wt, (qt, kt, vt))
    keep = same_position()
    attention(qt, kt, vt, acc0, ot, keep)
    at[TIME] = ot[...].T
    shared_t = share_forward(TIME)
    exchange_wait(0, dyb, dyr, own_dy)
    dy = from_blocks(dyr)
    dyf[TIME, :TOK, :] = dy
    shared_t.append(share(dyf, TIME))
    da[:, :HD] = dot(dy, pt[...], NT).astype(BF16)
    da[:, HD:] = jnp.zeros((TOK, PAD - HD), BF16)
    accs = (acc0, acc1, acc2)
    attention_back(qt, kt, vt, ot, da, accs, keep, {})
    pack(accs, dpk.at[TIME, pl.ds(0, TOK)])
    shared_t.append(share(dpk, TIME))
    middle = from_blocks(nxr).astype(F32)
    to_blocks(block_back(dy, middle, wt, dpk.at[TIME, pl.ds(0, TOK)]).astype(BF16), dxb)
    own_dx = exchange_start(2, dxb, dxr)

    first_t, second_t = rings(TIME)
    weight_terms(TIME, shared_t)
    for r in first_t:
        r.first()

    exchange_wait(2, dxb, dxr, own_dx)
    dy = from_blocks(dxr)
    dyf[SPACE, :TOK, :] = dy
    shared_s.append(share(dyf, SPACE))
    da[:, :HD] = dot(dy, ps[...], NT).astype(BF16)

    def hook_second():
        for r in first_t:
            r.second()

    def hook_between():
        between(TIME, first_t, second_t)

    attention_back(qs, ks, vs, os, da, accs, None, {0: hook_second, 5: hook_between})
    pack(accs, dpk.at[SPACE, pl.ds(0, TOK)])
    shared_s.append(share(dpk, SPACE))
    for r in second_t:
        r.second()
    dx_out[...] = block_back(dy, x_v[...].astype(F32), ws, dpk.at[SPACE, pl.ds(0, TOK)]).astype(BF16)
    first_s, second_s = rings(SPACE)
    weight_terms(SPACE, shared_s)
    for r in first_s:
        r.first()
    along = last(TIME, second_t)
    for r in first_s:
        r.second()
    finish(TIME, along, gqt, gpt)
    between(SPACE, first_s, second_s)
    for r in second_s:
        r.second()
    finish(SPACE, last(SPACE, second_s), gqs, gps)


def per_device(latents, out_grad, qkv_spatial, proj_spatial, qkv_temporal, proj_temporal):
    ins = [latents[0, 0], out_grad[0, 0], qkv_spatial, proj_spatial.T, qkv_temporal, proj_temporal.T]
    wide, narrow = VMEM((TOK, D), BF16), VMEM((TOK, PAD), BF16)
    qkv, proj = VMEM((3 * HD, D), BF16), VMEM((HD, D), BF16)
    blocks = VMEM((GROUPS, D // 128, OWN, 128), BF16)
    acc = VMEM((TOK, PAD), F32)
    terms = VMEM((2, 4, 2, 2, PART, 256), BF16)
    half = PART // 2
    dma = pltpu.SemaphoreType.DMA
    f32 = [jax.ShapeDtypeStruct(s, F32) for s in ((27, 288), (18, 144), (27, 288), (18, 144))]
    outs = [jax.ShapeDtypeStruct((TOK, D), BF16), *f32]
    dx, qkv_s, proj_s, qkv_t, proj_t = pl.pallas_call(
        kernel,
        out_shape=outs,
        in_specs=[pl.BlockSpec(memory_space=pl.ANY)] * len(ins),
        out_specs=[pl.BlockSpec(memory_space=VMEM)] * len(outs),
        scratch_shapes=[
            wide, wide, qkv, proj, qkv, proj,
            *[blocks] * 6,
            *[narrow] * 9, acc, acc, acc,
            VMEM((2, D, TOK), BF16),
            VMEM((2, PAD, TOK), BF16),
            VMEM((2, 2 * QROWS, 2 * TOK), BF16),
            VMEM((2, 192, 2 * TOK), BF16),
            VMEM((2, 96, 2 * TOK), BF16),
            VMEM((2, 2 * TOK, 3 * PAD), BF16),
            VMEM((2, 2 * TOK, D), BF16),
            VMEM((TILES, QWIN, 128), BF16),
            VMEM((TILES, PWIN, 384), BF16),
            VMEM((2 * TOK, 512), BF16),
            VMEM((3, 2 * TOK, 512), BF16),
            terms, terms,
            *[VMEM((2, 2, 2, PART, 256), BF16)] * 2,
            *[VMEM((2, 2, 2, 2, PART, 256), BF16)] * 2,
            *[VMEM((2, 4, PART, 256), BF16)] * 2,
            *[VMEM((2, 2, half, 256), BF16)] * 2,
            *[VMEM((2, 2, 2, half, 256), BF16)] * 2,
            *[VMEM((2, 8, 32, ROWS), BF16)] * 2,
            dma((78,)), dma((78,)), dma((3,)), dma((3,)), dma((9,)),
        ],
        name="both_blocks",
        compiler_params=pltpu.CompilerParams(
            collective_id=0, has_side_effects=True, vmem_limit_bytes=LIMIT
        ),
    )(*ins)
    return dx[None, None], qkv_s, proj_s, qkv_t, proj_t


def solution(mesh):
    placed = (P("dp", "seq", None, None), P("dp", "seq", None, None), P(), P(), P(), P())
    return jax.shard_map(
        per_device,
        mesh=mesh,
        in_specs=placed,
        out_specs=(
            P("dp", "seq", None, None),
            P("seq", "dp"),
            P("seq", "dp"),
            P("seq", "dp"),
            P("seq", "dp"),
        ),
        check_vma=False,
    )
```

time: 564 us -> 127 us (0.23)
  the two profiles are of different devices: /device:TPU:1 before, /device:TPU:8 now
where the time goes in v1:
time: 127 us; the launch traced here: 126 us
  Pallas kernels  118 us (93%)
  local copies, waits for them, and re-layouts  7.46 us (6%)
    pallas_call x1, Pallas kernels, per_device(): pl.pallas_call(kernel, out_shape=outs, in_specs=[pl.BlockSpec(memory_spac...  118 us
    unnamed x5, local copies, waits for them, and re-layouts  7.46 us

profile of v1, /device:TPU:8, one launch (start us, length us, event | category | flops | bytes accessed | tf_op | source)
XLA Modules:
  0.0 126.4 jit_solution(11329358832432576147)
XLA Ops:
  0.6 118.3 %both_blocks.1 = (bf16[256,1152]{1,0:T(8,128)(2,1)}, f32[27,288]{1,0:T(8,128)}, f32[18,144]{1,0:T(8,128)}, f32[27,288]{1,0:T(8,128)}, f32[18,144]{1,0:T(8,128)}) custom-call(bf16[256,1152]{1,0:T(8,128)(2,1)} %bitcast.7, bf16[256,1152]{1,0:T(8,128)(2,1)} %bitcast.8, bf16[1728,1152]{1,0:T(8,128)(2,1)} %ws_in.1, bf16[576,1152]{1,0:T(8,128)(2,1)} %bitcast.5, ...), custom_call_target="tpu_custom_call" | custom-call | tf_op jit(solution)/shard_map/both_blocks/pallas_call | solution.py:493
  119.0 1.9 %copy.16 = bf16[1,1,256,1152]{3,2,1,0:T(8,128)(2,1)} copy(bf16[1,1,256,1152]{3,2,1,0:T(8,128)(2,1)} %bitcast.9) | data formatting | bytes 1179648
  120.9 1.4 %copy.17 = f32[27,288]{1,0:T(8,128)} copy(f32[27,288]{1,0:T(8,128)} %get-tuple-element.21) | data formatting | bytes 62208
  122.3 1.3 %copy.18 = f32[18,144]{1,0:T(8,128)} copy(f32[18,144]{1,0:T(8,128)} %get-tuple-element.22) | data formatting | bytes 20736
  123.7 1.4 %copy.19 = f32[27,288]{1,0:T(8,128)} copy(f32[27,288]{1,0:T(8,128)} %get-tuple-element.23) | data formatting | bytes 62208
  125.1 1.3 %copy.20 = f32[18,144]{1,0:T(8,128)} copy(f32[18,144]{1,0:T(8,128)} %get-tuple-element.24) | data formatting | bytes 20736

commit v2 on v1

--- a/solution.py
+++ b/solution.py
@@ -25,7 +25,7 @@
 QROWS = 288
 PROWS = 96
 ROWS = QROWS + PROWS
-PART = ROWS // 2
+PARTS = ((144, True), (144, False), (48, True), (48, False))
 TILES = 16
 QWIN = 384
 PWIN = 256
@@ -110,23 +110,23 @@
         dpk[:, i * PAD : (i + 1) * PAD] = acc[...].astype(BF16)
 
 
-def block_back(dy, x, w_ref, dpk):
+def block_back(x, w_ref, dpk):
     d_hidden = jnp.zeros((TOK, D), F32)
     for i in range(3):
         part = dpk[:, i * PAD : i * PAD + HD]
         d_hidden = d_hidden + dot(part, w_ref[i * HD : (i + 1) * HD, :])
     normed, inverse = normalize(x)
     along = jnp.mean(d_hidden * normed, axis=-1, keepdims=True)
-    return dy.astype(F32) + inverse * (d_hidden - normed * along)
+    return inverse * (d_hidden - normed * along)
 
 
 def to_blocks(value, ref):
-    for t in range(D // 128):
+    for t in range(ref.shape[1]):
         ref[:, t, :, :] = value[:, t * 128 : (t + 1) * 128].reshape(GROUPS, OWN, 128)
 
 
 def from_blocks(ref):
-    return jnp.concatenate([ref[:, t, :, :].reshape(TOK, 128) for t in range(D // 128)], axis=1)
+    return jnp.concatenate([ref[:, t, :, :].reshape(TOK, 128) for t in range(ref.shape[1])], axis=1)
 
 
 def at_xyz(x, y, z, core):
@@ -170,29 +170,37 @@
         ps[tile, :, 256:384] = choice(low, PWIN, 18 * shard + 9, 18, 9, 36, ())
 
 
-def gradients(qs, ps, hcat, a01, a2, dpk, dy, mq, mp, ga, gb):
+def qkv_terms(qs, hcat, dpk, mq, g):
     for x in range(4):
         for t in range(4):
-            tile, here = x * 4 + t, slice(t * 128, (t + 1) * 128)
+            tile = x * 4 + t
             low = qlow(tile)
-            mq[:, here] = dot(dpk[:, low : low + QWIN], qs[tile]).astype(BF16)
+            spread = dot(dpk[:, low : low + QWIN], qs[tile])
+            mq[:, t * 128 : (t + 1) * 128] = spread.astype(BF16)
+        total = dot(hcat[...], mq[...]).astype(BF16)
+        for y_lo in range(2):
+            for y_hi in range(2):
+                for p in range(2):
+                    row = y_lo * QROWS + p * 144
+                    g[p][x, y_hi, y_lo] = total[row : row + 144, y_hi * 256 : (y_hi + 1) * 256]
+
+
+def proj_terms(ps, a01, a2, dy, mp, g):
+    for x in range(4):
+        for t in range(4):
+            tile = x * 4 + t
             low = plow(tile)
             spread = dot(dy[:, low : low + PWIN], ps[tile]).astype(BF16)
             for j in range(3):
-                mp[j, :, here] = spread[:, j * 128 : (j + 1) * 128]
-        qkv = dot(hcat[...], mq[...])
-        proj = dot(a01[...], mp[0])
-        last = [dot(a2[...], mp[1]), dot(a2[...], mp[2])]
-        for y_lo in range(2):
-            for y_hi in range(2):
-                here = slice(y_hi * 256, (y_hi + 1) * 256)
-                row = y_lo * QROWS
-                ga[x, y_hi, y_lo] = qkv[row : row + PART, here].astype(BF16)
-                gb[x, y_hi, y_lo, 0:96] = qkv[row + PART : row + QROWS, here].astype(BF16)
-                for g in range(2):
-                    both = proj[y_lo * 96 + g * 48 : y_lo * 96 + g * 48 + 48, here]
-                    both = both + last[g][y_lo * 48 : y_lo * 48 + 48, here]
-                    gb[x, y_hi, y_lo, 96 + 48 * g : 144 + 48 * g] = both.astype(BF16)
+                mp[j, :, t * 128 : (t + 1) * 128] = spread[:, j * 128 : (j + 1) * 128]
+        most = dot(a01[...], mp[0])
+        for p in range(2):
+            last = dot(a2[...], mp[1 + p])
+            for y_lo in range(2):
+                row = y_lo * 96 + p * 48
+                total = (most[row : row + 48] + last[y_lo * 48 : y_lo * 48 + 48]).astype(BF16)
+                for y_hi in range(2):
+                    g[2 + p][x, y_hi, y_lo] = total[:, y_hi * 256 : (y_hi + 1) * 256]
 
 
 class Ring:
@@ -229,18 +237,58 @@
         return own.astype(F32) + near.reshape(own.shape)
 
 
+class Part:
+    def __init__(self, copy, refs, rows, x_first, position, along_x, along_y):
+        self.copy, self.rows, self.x_first = copy, rows, x_first
+        self.g, relay, near, self.h, self.r = refs
+        self.x, self.y_hi, self.y_lo = position
+        y = self.y_hi * 2 + self.y_lo
+        if x_first:
+            self.ring = Ring(copy, self.of_x, relay, near, self.x, along_x)
+            self.other, self.along = y, along_y
+        else:
+            self.ring = Ring(copy, self.of_y, relay, near, y, along_y)
+            self.other, self.along = self.x, along_x
+
+    def of_x(self, i, half):
+        return self.g.at[i, half]
+
+    def of_y(self, i, half):
+        return self.g.at[pl.ds(2 * half, 2), lax.div(i, 2), lax.rem(i, 2)]
+
+    def first(self):
+        self.ring.first()
+
+    def second(self):
+        self.ring.second()
+
+    def across(self):
+        own = self.g[self.x] if self.x_first else self.g[:, self.y_hi, self.y_lo]
+        self.h[...] = self.ring.total(own.reshape(4, self.rows, 256)).astype(BF16)
+        self.copies = [
+            self.copy(self.h.at[lax.rem(self.other + k, 4)], self.r.at[k], self.along(k))
+            for k in range(1, 4)
+        ]
+
+    def total(self):
+        acc = self.h[self.other].astype(F32)
+        for k, c in enumerate(self.copies):
+            c.wait()
+            acc = acc + self.r[k + 1].astype(F32)
+        return acc
+
+
 def kernel(
     x_in, dy_in, ws_in, ps_in, wt_in, pt_in,
-    dx_out, gqs, gps, gqt, gpt,
+    dx_out, sums_out,
     x_v, dy_v, ws, ps, wt, pt,
-    dyb, dyr, nxb, nxr, dxb, dxr,
+    nxb, nxr, dxb, dxr, dab, dar, otb, otr,
     qs, ks, vs, os, qt, kt, vt, ot, da, acc0, acc1, acc2,
     ht, at, hcat, a01, a2, dpk, dyf,
     spread_q, spread_p, mq, mp,
-    ga, gb, relay_a, relay_b, near_a, near_b,
-    ha, hb, relay2_a, relay2_b, near2_a, near2_b,
     zs, zr,
     send, recv, all_send, all_recv, local,
+    *part_refs,
 ):
     dp, me = lax.axis_index("dp"), lax.axis_index("seq")
     core, y_lo = lax.rem(dp, 2), lax.div(dp, 2)
@@ -280,12 +328,12 @@
         c.start()
         return c
 
-    get_dy = here(dy_in, dy_v)
     get_x = here(x_in, x_v)
     get_ws = here(ws_in, ws)
     get_ps = here(ps_in, ps)
+    get_dy = here(dy_in, dy_v)
+    get_pt = here(pt_in, pt)
     get_wt = here(wt_in, wt)
-    get_pt = here(pt_in, pt)
 
     barrier = pltpu.get_barrier_semaphore()
 
@@ -324,82 +372,61 @@
 
     far = pl.ds(TOK, TOK)
 
-    def share_forward(b):
+    def share_hidden(b):
         copies = []
         for i in range(2):
-            block = i * 2 + 1 - core
-            rows = pl.ds(pl.multiple_of(block * QROWS, 32), QROWS)
+            rows = pl.ds(pl.multiple_of((i * 2 + 1 - core) * QROWS, 32), QROWS)
             copies.append(copy(ht.at[b, rows], hcat.at[b, pl.ds(i * QROWS, QROWS), far], pair))
-            rows = pl.ds(pl.multiple_of(block * 144, 16), 96)
+            rows = pl.ds(pl.multiple_of((i * 2 + core) * QROWS, 32), QROWS)
+            hcat[b, i * QROWS : (i + 1) * QROWS, :TOK] = ht[b, rows, :]
+        return copies
+
+    def share_attn(b):
+        copies = []
+        for i in range(2):
+            row = (i * 2 + 1 - core) * 144
+            rows = pl.ds(pl.multiple_of(row, 16), 96)
             copies.append(copy(at.at[b, rows], a01.at[b, pl.ds(i * 96, 96), far], pair))
-            rows = pl.ds(pl.multiple_of(block * 144 + 96, 16), 48)
+            rows = pl.ds(pl.multiple_of(row + 96, 16), 48)
             copies.append(copy(at.at[b, rows], a2.at[b, pl.ds(i * 48, 48), far], pair))
-            block = i * 2 + core
-            rows = pl.ds(pl.multiple_of(block * QROWS, 32), QROWS)
-            hcat[b, i * QROWS : (i + 1) * QROWS, :TOK] = ht[b, rows, :]
-            rows = pl.ds(pl.multiple_of(block * 144, 16), 96)
+            row = (i * 2 + core) * 144
+            rows = pl.ds(pl.multiple_of(row, 16), 96)
             a01[b, i * 96 : (i + 1) * 96, :TOK] = at[b, rows, :]
-            rows = pl.ds(pl.multiple_of(block * 144 + 96, 16), 48)
+            rows = pl.ds(pl.multiple_of(row + 96, 16), 48)
             a2[b, i * 48 : (i + 1) * 48, :TOK] = at[b, rows, :]
         return copies
 
     def share(ref, b):
         return copy(ref.at[b, pl.ds(0, TOK)], ref.at[b, far], pair)
 
-    def rings(b):
-        first = (
-            Ring(copy, lambda i, h: ga.at[b, i, h], relay_a.at[b], near_a.at[b], x, along_x),
-            Ring(
-                copy,
-                lambda i, h: gb.at[b, pl.ds(2 * h, 2), lax.div(i, 2), lax.rem(i, 2)],
-                relay_b.at[b], near_b.at[b], y, along_y,
-            ),
-        )
-        half = PART // 2
-        second = (
-            Ring(copy, lambda i, h: ha.at[b, i, pl.ds(h * half, half)], relay2_a.at[b], near2_a.at[b], y, along_y),
-            Ring(copy, lambda i, h: hb.at[b, i, pl.ds(h * half, half)], relay2_b.at[b], near2_b.at[b], x, along_x),
-        )
-        return first, second
-
-    def weight_terms(b, copies):
+    def parts(b):
+        found = []
+        for p, (rows, x_first) in enumerate(PARTS):
+            refs = [ref.at[b] for ref in part_refs[p * 5 : (p + 1) * 5]]
+            found.append(Part(copy, refs, rows, x_first, (x, y_hi, y_lo), along_x, along_y))
+        return found
+
+    def wait(copies):
         for c in copies:
             c.wait()
-        gradients(
-            spread_q, spread_p, hcat.at[b], a01.at[b], a2.at[b], dpk.at[b], dyf.at[b], mq, mp, ga.at[b], gb.at[b]
-        )
-
-    def between(b, first, second):
-        ha[b] = first[0].total(ga[b, x].reshape(4, PART, 256)).astype(BF16)
-        second[0].first()
-        hb[b] = first[1].total(gb[b, :, y_hi, y_lo]).astype(BF16)
-        second[1].first()
-
-    def last(b, second):
-        sums = [second[0].total(ha[b, y]), second[1].total(hb[b, x])]
-        sums = jnp.concatenate(sums, axis=0).T
-        zs[b] = sums.reshape(8, 32, ROWS).astype(BF16)
-        copies = []
-        for k in range(1, 8):
-            copies.append(copy(zs.at[b, lax.rem(z + k, 8)], zr.at[b, k], along_z(k)))
-        return copies
-
-    def finish(b, copies, qkv, proj):
+
+    def last(b, found):
+        total = jnp.concatenate([p.total() for p in found], axis=0).T
+        zs[b] = total.reshape(8, 32, ROWS).astype(BF16)
+        return [copy(zs.at[b, lax.rem(z + k, 8)], zr.at[b, k], along_z(k)) for k in range(1, 8)]
+
+    def finish(b, copies):
         acc = zs[b, z].astype(F32)
         for k in range(1, 8):
             copies[k - 1].wait()
             acc = acc + zr[b, k].astype(F32)
-        qkv[...] = acc[:27, :QROWS]
-        proj[:, 0:96] = acc[:18, QROWS:]
-        proj[0:9, 96:144] = acc[18:27, QROWS : QROWS + 48]
-        proj[9:18, 96:144] = acc[18:27, QROWS + 48 :]
+        sums_out[b] = acc
 
     SPACE, TIME = 0, 1
-
-    get_dy.wait()
-    to_blocks(dy_v[...], dyb)
-    pl.semaphore_wait(barrier, n + 2)
-    own_dy = exchange_start(0, dyb, dyr)
+    space, time = parts(SPACE), parts(TIME)
+    own = pl.ds(0, TOK)
+    accs = (acc0, acc1, acc2)
+
     get_x.wait()
     source = x_v[...].astype(F32)
     normed, _ = normalize(source)
@@ -409,74 +436,108 @@
     attention(qs, ks, vs, acc0, os, None)
     get_ps.wait()
     to_blocks((source + dot(os[:, :HD], ps[...])).astype(BF16), nxb)
-    own_next = exchange_start(1, nxb, nxr)
+    get_dy.wait()
+    get_pt.wait()
+    dyf[TIME, :TOK, :] = dy_v[...]
+    da[:, :HD] = dot(dy_v[...], pt[...], NT).astype(BF16)
+    da[:, HD:] = jnp.zeros((TOK, PAD - HD), BF16)
+    to_blocks(da[...], dab)
+    pl.semaphore_wait(barrier, n + 2)
+    own_next = exchange_start(0, nxb, nxr)
+    own_da = exchange_start(1, dab, dar)
     ht[SPACE] = hidden.T
     at[SPACE] = os[...].T
-    shared_s = share_forward(SPACE)
+    hidden_s = share_hidden(SPACE)
+    proj_s = share_attn(SPACE)
+    proj_t = [share(dyf, TIME)]
     spreaders(spread_q, spread_p)
 
     get_wt.wait()
-    get_pt.wait()
-    exchange_wait(1, nxb, nxr, own_next)
-    middle = from_blocks(nxr)
-    normed, _ = normalize(middle.astype(F32))
+    exchange_wait(0, nxb, nxr, own_next)
+    normed, _ = normalize(from_blocks(nxr).astype(F32))
     hidden = normed.astype(BF16)
-    ht[TIME] = hidden.T
     project(hidden, wt, (qt, kt, vt))
     keep = same_position()
     attention(qt, kt, vt, acc0, ot, keep)
-    at[TIME] = ot[...].T
-    shared_t = share_forward(TIME)
-    exchange_wait(0, dyb, dyr, own_dy)
-    dy = from_blocks(dyr)
-    dyf[TIME, :TOK, :] = dy
-    shared_t.append(share(dyf, TIME))
-    da[:, :HD] = dot(dy, pt[...], NT).astype(BF16)
+    to_blocks(ot[...], otb)
+    own_attn = exchange_start(3, otb, otr)
+    ht[TIME] = hidden.T
+    hidden_t = share_hidden(TIME)
+    exchange_wait(1, dab, dar, own_da)
+    da[...] = from_blocks(dar)
+    attention_back(qt, kt, vt, ot, da, accs, keep, {})
+    pack(accs, dpk.at[TIME, own])
+    hidden_t.append(share(dpk, TIME))
+    middle = from_blocks(nxr).astype(F32)
+    to_blocks(block_back(middle, wt, dpk.at[TIME, own]).astype(BF16), dxb)
+    own_dx = exchange_start(2, dxb, dxr)
+
+    wait(hidden_t)
+    qkv_terms(spread_q, hcat.at[TIME], dpk.at[TIME], mq, [p.g for p in time])
+    time[0].first()
+    time[1].first()
+    exchange_wait(3, otb, otr, own_attn)
+    at[TIME] = from_blocks(otr).T
+    proj_t += share_attn(TIME)
+    wait(proj_t)
+    proj_terms(spread_p, a01.at[TIME], a2.at[TIME], dyf.at[TIME], mp, [p.g for p in time])
+    time[2].first()
+    time[3].first()
+
+    exchange_wait(2, dxb, dxr, own_dx)
+    dy = (dy_v[...].astype(F32) + from_blocks(dxr).astype(F32)).astype(BF16)
+    dyf[SPACE, :TOK, :] = dy
+    proj_s.append(share(dyf, SPACE))
+    da[:, :HD] = dot(dy, ps[...], NT).astype(BF16)
     da[:, HD:] = jnp.zeros((TOK, PAD - HD), BF16)
-    accs = (acc0, acc1, acc2)
-    attention_back(qt, kt, vt, ot, da, accs, keep, {})
-    pack(accs, dpk.at[TIME, pl.ds(0, TOK)])
-    shared_t.append(share(dpk, TIME))
-    middle = from_blocks(nxr).astype(F32)
-    to_blocks(block_back(dy, middle, wt, dpk.at[TIME, pl.ds(0, TOK)]).astype(BF16), dxb)
-    own_dx = exchange_start(2, dxb, dxr)
-
-    first_t, second_t = rings(TIME)
-    weight_terms(TIME, shared_t)
-    for r in first_t:
-        r.first()
-
-    exchange_wait(2, dxb, dxr, own_dx)
-    dy = from_blocks(dxr)
-    dyf[SPACE, :TOK, :] = dy
-    shared_s.append(share(dyf, SPACE))
-    da[:, :HD] = dot(dy, ps[...], NT).astype(BF16)
-
-    def hook_second():
-        for r in first_t:
-            r.second()
-
-    def hook_between():
-        between(TIME, first_t, second_t)
-
-    attention_back(qs, ks, vs, os, da, accs, None, {0: hook_second, 5: hook_between})
-    pack(accs, dpk.at[SPACE, pl.ds(0, TOK)])
-    shared_s.append(share(dpk, SPACE))
-    for r in second_t:
-        r.second()
-    dx_out[...] = block_back(dy, x_v[...].astype(F32), ws, dpk.at[SPACE, pl.ds(0, TOK)]).astype(BF16)
-    first_s, second_s = rings(SPACE)
-    weight_terms(SPACE, shared_s)
-    for r in first_s:
-        r.first()
-    along = last(TIME, second_t)
-    for r in first_s:
-        r.second()
-    finish(TIME, along, gqt, gpt)
-    between(SPACE, first_s, second_s)
-    for r in second_s:
-        r.second()
-    finish(SPACE, last(SPACE, second_s), gqs, gps)
+
+    def hook_a():
+        time[0].second()
+        time[1].second()
+
+    def hook_b():
+        wait(proj_s)
+        proj_terms(spread_p, a01.at[SPACE], a2.at[SPACE], dyf.at[SPACE], mp, [p.g for p in space])
+        space[2].first()
+        space[3].first()
+
+    def hook_c():
+        time[2].second()
+        time[3].second()
+
+    hooks = {0: hook_a, 3: hook_b, 6: hook_c}
+    attention_back(qs, ks, vs, os, da, accs, None, hooks)
+    pack(accs, dpk.at[SPACE, own])
+    hidden_s.append(share(dpk, SPACE))
+    for p in time:
+        p.across()
+    wait(hidden_s)
+    qkv_terms(spread_q, hcat.at[SPACE], dpk.at[SPACE], mq, [p.g for p in space])
+    space[0].first()
+    space[1].first()
+    space[2].second()
+    space[3].second()
+    along = last(TIME, time)
+    dx_s = block_back(x_v[...].astype(F32), ws, dpk.at[SPACE, own])
+    dx_out[...] = (dyf[SPACE, :TOK, :].astype(F32) + dx_s).astype(BF16)
+    space[0].second()
+    space[1].second()
+    space[2].across()
+    space[3].across()
+    finish(TIME, along)
+    space[0].across()
+    space[1].across()
+    finish(SPACE, last(SPACE, space))
+
+
+def outputs_kernel(dx, sums, dx_out, gqs, gps, gqt, gpt):
+    dx_out[...] = dx[...]
+    for b, (qkv, proj) in enumerate(((gqs, gps), (gqt, gpt))):
+        block = sums[b]
+        qkv[...] = block[:27, :QROWS]
+        proj[:, 0:96] = block[:18, QROWS:]
+        proj[0:9, 96:144] = block[18:27, QROWS : QROWS + 48]
+        proj[9:18, 96:144] = block[18:27, QROWS + 48 :]
 
 
 def per_device(latents, out_grad, qkv_spatial, proj_spatial, qkv_temporal, proj_temporal):
@@ -484,20 +545,29 @@
     wide, narrow = VMEM((TOK, D), BF16), VMEM((TOK, PAD), BF16)
     qkv, proj = VMEM((3 * HD, D), BF16), VMEM((HD, D), BF16)
     blocks = VMEM((GROUPS, D // 128, OWN, 128), BF16)
+    small = VMEM((GROUPS, PAD // 128, OWN, 128), BF16)
     acc = VMEM((TOK, PAD), F32)
-    terms = VMEM((2, 4, 2, 2, PART, 256), BF16)
-    half = PART // 2
     dma = pltpu.SemaphoreType.DMA
-    f32 = [jax.ShapeDtypeStruct(s, F32) for s in ((27, 288), (18, 144), (27, 288), (18, 144))]
-    outs = [jax.ShapeDtypeStruct((TOK, D), BF16), *f32]
-    dx, qkv_s, proj_s, qkv_t, proj_t = pl.pallas_call(
+    part_refs = []
+    for rows, _ in PARTS:
+        part_refs += [
+            VMEM((2, 4, 2, 2, rows, 256), BF16),
+            VMEM((2, 2, 2, rows, 256), BF16),
+            VMEM((2, 2, 2, 2, rows, 256), BF16),
+            VMEM((2, 4, rows, 256), BF16),
+            VMEM((2, 4, rows, 256), BF16),
+        ]
+    dx, sums = pl.pallas_call(
         kernel,
-        out_shape=outs,
+        out_shape=[
+            jax.ShapeDtypeStruct((TOK, D), BF16),
+            jax.ShapeDtypeStruct((2, 32, ROWS), F32),
+        ],
         in_specs=[pl.BlockSpec(memory_space=pl.ANY)] * len(ins),
-        out_specs=[pl.BlockSpec(memory_space=VMEM)] * len(outs),
+        out_specs=[pl.BlockSpec(memory_space=VMEM)] * 2,
         scratch_shapes=[
             wide, wide, qkv, proj, qkv, proj,
-            *[blocks] * 6,
+            *[blocks] * 4, *[small] * 4,
             *[narrow] * 9, acc, acc, acc,
             VMEM((2, D, TOK), BF16),
             VMEM((2, PAD, TOK), BF16),
@@ -510,20 +580,24 @@
             VMEM((TILES, PWIN, 384), BF16),
             VMEM((2 * TOK, 512), BF16),
             VMEM((3, 2 * TOK, 512), BF16),
-            terms, terms,
-            *[VMEM((2, 2, 2, PART, 256), BF16)] * 2,
-            *[VMEM((2, 2, 2, 2, PART, 256), BF16)] * 2,
-            *[VMEM((2, 4, PART, 256), BF16)] * 2,
-            *[VMEM((2, 2, half, 256), BF16)] * 2,
-            *[VMEM((2, 2, 2, half, 256), BF16)] * 2,
             *[VMEM((2, 8, 32, ROWS), BF16)] * 2,
-            dma((78,)), dma((78,)), dma((3,)), dma((3,)), dma((9,)),
+            dma((102,)), dma((102,)), dma((4,)), dma((4,)), dma((10,)),
+            *part_refs,
         ],
         name="both_blocks",
         compiler_params=pltpu.CompilerParams(
             collective_id=0, has_side_effects=True, vmem_limit_bytes=LIMIT
         ),
     )(*ins)
+    vmem = pl.BlockSpec(memory_space=VMEM)
+    f32 = [jax.ShapeDtypeStruct(s, F32) for s in ((27, 288), (18, 144), (27, 288), (18, 144))]
+    dx, qkv_s, proj_s, qkv_t, proj_t = pl.pallas_call(
+        outputs_kernel,
+        out_shape=[jax.ShapeDtypeStruct((TOK, D), BF16), *f32],
+        in_specs=[vmem] * 2,
+        out_specs=[vmem] * 5,
+        name="outputs",
+    )(dx, sums)
     return dx[None, None], qkv_s, proj_s, qkv_t, proj_t
 
 

time: 127 us -> 108 us (0.85)
  Pallas kernels: 118 us -> 107 us
  local copies, waits for them, and re-layouts: 7.46 us -> 0 us
    pallas_call x1 -> x2, Pallas kernels: 118 us -> 107 us  [the longest x1 105 us: per_device(): pl.pallas_call(kernel, out_shape=[jax.ShapeDtypeStruct((TOK, D), BF16), j...]
    unnamed x5 -> x0, local copies, waits for them, and re-layouts: 7.46 us -> none
where the time goes in v2:
time: 108 us
  Pallas kernels  107 us (99%)
    pallas_call x1, Pallas kernels, per_device(): pl.pallas_call(kernel, out_shape=[jax.ShapeDtypeStruct((TOK, D), BF16), j...  105 us

profile of v2, /device:TPU:8, one launch (start us, length us, event | category | flops | bytes accessed | tf_op | source)
XLA Modules:
  0.0 108.0 jit_solution(5160549101070958662)
XLA Ops:
  0.6 105.5 %both_blocks.1 = (bf16[256,1152]{1,0:T(8,128)(2,1)}, f32[2,32,384]{2,1,0:T(8,128)}) custom-call(bf16[256,1152]{1,0:T(8,128)(2,1)} %bitcast.7, bf16[256,1152]{1,0:T(8,128)(2,1)} %bitcast.8, bf16[1728,1152]{1,0:T(8,128)(2,1)} %ws_in.1, bf16[576,1152]{1,0:T(8,128)(2,1)} %bitcast.5, bf16[1728,1152]{1,0:T(8,128)(2,1)} %wt_in.1, bf16[576,1152]{1,0:T(8,128)(2,1)} %bitcast.6), custom_call_target="tpu_custom_call" | custom-call | tf_op jit(solution)/shard_map/both_blocks/pallas_call | solution.py:560
  106.1 1.9 %outputs.1 = (bf16[256,1152]{1,0:T(8,128)(2,1)}, f32[27,288]{1,0:T(8,128)}, f32[18,144]{1,0:T(8,128)}, f32[27,288]{1,0:T(8,128)}, f32[18,144]{1,0:T(8,128)}) custom-call(bf16[256,1152]{1,0:T(8,128)(2,1)} %get-tuple-element.12.dx, f32[2,32,384]{2,1,0:T(8,128)} %get-tuple-element.13.sums), custom_call_target="tpu_custom_call" | custom-call | tf_op jit(solution)/shard_map/outputs/pallas_call | solution.py:594

commit v3 on v2

--- a/solution.py
+++ b/solution.py
@@ -25,10 +25,12 @@
 QROWS = 288
 PROWS = 96
 ROWS = QROWS + PROWS
-PARTS = ((144, True), (144, False), (48, True), (48, False))
+PARTS = ((80, True), (80, False), (64, True), (64, False), (48, True), (48, False))
+WAVES = ((0, 160), (160, 128))
 TILES = 16
 QWIN = 384
 PWIN = 256
+WIDE = 1792
 
 
 def dot(a, b, dims=((1,), (0,))):
@@ -74,17 +76,18 @@
     return lax.rem(rows, OWN) == lax.rem(columns, OWN)
 
 
-def attention(q, k, v, acc, attn, keep):
+def attention(q, k, v, acc, attn, kept, keep):
     acc[...] = jnp.zeros_like(acc)
     for h in range(HEADS):
         low, high = window(h)
         mask = head_mask(h, low, high)
         probs = softmax(q[:, low:high] * mask, k[:, low:high], keep)
-        acc[:, low:high] += dot(probs.astype(BF16), v[:, low:high] * mask)
+        kept[h] = probs.astype(BF16)
+        acc[:, low:high] += dot(kept[h], v[:, low:high] * mask)
     attn[...] = acc[...].astype(BF16)
 
 
-def attention_back(q, k, v, attn, da, accs, keep, hooks):
+def attention_back(q, k, v, attn, da, accs, kept, hooks):
     for acc in accs:
         acc[...] = jnp.zeros_like(acc)
     dq, dk, dv = accs
@@ -96,25 +99,22 @@
         qm = q[:, low:high] * mask
         km = k[:, low:high] * mask
         dam = da[:, low:high] * mask
-        probs = softmax(qm, k[:, low:high], keep)
         d_probs = dot(dam, v[:, low:high], NT)
-        dv[:, low:high] += dot(probs.astype(BF16), dam, TN)
+        dv[:, low:high] += dot(kept[h], dam, TN)
         offset = jnp.sum(dam.astype(F32) * attn[:, low:high].astype(F32), axis=-1, keepdims=True)
-        ds = (probs * (d_probs - offset) * SCALE).astype(BF16)
+        ds = (kept[h].astype(F32) * ((d_probs - offset) * SCALE)).astype(BF16)
         dq[:, low:high] += dot(ds, km)
         dk[:, low:high] += dot(ds, qm, TN)
 
 
 def pack(accs, dpk):
     for i, acc in enumerate(accs):
-        dpk[:, i * PAD : (i + 1) * PAD] = acc[...].astype(BF16)
+        dpk[:, i * HD : (i + 1) * HD] = acc[:, :HD].astype(BF16)
+    dpk[:, 3 * HD :] = jnp.zeros((TOK, WIDE - 3 * HD), BF16)
 
 
 def block_back(x, w_ref, dpk):
-    d_hidden = jnp.zeros((TOK, D), F32)
-    for i in range(3):
-        part = dpk[:, i * PAD : i * PAD + HD]
-        d_hidden = d_hidden + dot(part, w_ref[i * HD : (i + 1) * HD, :])
+    d_hidden = dot(dpk[:, : 3 * HD], w_ref[...])
     normed, inverse = normalize(x)
     along = jnp.mean(d_hidden * normed, axis=-1, keepdims=True)
     return inverse * (d_hidden - normed * along)
@@ -138,51 +138,51 @@
     return [(x * 8 + z_hi * 4 + i) * 2 + y_hi for i in range(4)]
 
 
-def qplace(column):
-    return column + (PAD - HD) * (column // HD)
-
-
 def qlow(tile):
-    return min(qplace(27 * lane_shards(tile)[0]) // 128 * 128, 3 * PAD - QWIN)
+    return min(27 * lane_shards(tile)[0] // 128 * 128, WIDE - QWIN)
 
 
 def plow(tile):
     return min(18 * lane_shards(tile)[0] // 128 * 128, D - PWIN)
 
 
-def choice(low, window, lead, first, count, step, edges):
+def choice(low, window, lead, first, count, step):
     row = lax.broadcasted_iota(jnp.int32, (window, 128), 0) + low
     lane = lax.broadcasted_iota(jnp.int32, (1, 128), 1)
     inner = (lane & 31) - first
     wanted = lead + lax.shift_right_logical(lane, 5) * step + inner
-    gaps = sum((jnp.where(wanted >= e, PAD - HD, 0) for e in edges), jnp.zeros_like(wanted))
-    wanted = jnp.where((inner >= 0) & (inner < count), wanted + gaps, -1)
+    wanted = jnp.where((inner >= 0) & (inner < count), wanted, -1)
     return (row == wanted).astype(F32).astype(BF16)
 
 
 def spreaders(qs, ps):
     for tile in range(TILES):
         shard = lane_shards(tile)[0]
-        qs[tile] = choice(qlow(tile), QWIN, 27 * shard, 0, 27, 54, (HD, 2 * HD))
+        qs[tile] = choice(qlow(tile), QWIN, 27 * shard, 0, 27, 54)
         low = plow(tile)
-        ps[tile, :, 0:128] = choice(low, PWIN, 18 * shard, 0, 18, 36, ())
-        ps[tile, :, 128:256] = choice(low, PWIN, 18 * shard, 18, 9, 36, ())
-        ps[tile, :, 256:384] = choice(low, PWIN, 18 * shard + 9, 18, 9, 36, ())
-
-
-def qkv_terms(qs, hcat, dpk, mq, g):
+        ps[tile, :, 0:128] = choice(low, PWIN, 18 * shard, 0, 18, 36)
+        ps[tile, :, 128:256] = choice(low, PWIN, 18 * shard, 18, 9, 36)
+        ps[tile, :, 256:384] = choice(low, PWIN, 18 * shard + 9, 18, 9, 36)
+
+
+def qkv_spread(qs, dpk, mq):
+    for tile in range(TILES):
+        low = qlow(tile)
+        spread = dot(dpk[:, low : low + QWIN], qs[tile])
+        mq[:, tile * 128 : (tile + 1) * 128] = spread.astype(BF16)
+
+
+def qkv_terms(wave, hcat, mq, g):
+    first, rows = WAVES[wave]
     for x in range(4):
-        for t in range(4):
-            tile = x * 4 + t
-            low = qlow(tile)
-            spread = dot(dpk[:, low : low + QWIN], qs[tile])
-            mq[:, t * 128 : (t + 1) * 128] = spread.astype(BF16)
-        total = dot(hcat[...], mq[...]).astype(BF16)
+        total = dot(hcat[2 * first : 2 * (first + rows)], mq[:, x * 512 : (x + 1) * 512])
+        total = total.astype(BF16)
         for y_lo in range(2):
             for y_hi in range(2):
                 for p in range(2):
-                    row = y_lo * QROWS + p * 144
-                    g[p][x, y_hi, y_lo] = total[row : row + 144, y_hi * 256 : (y_hi + 1) * 256]
+                    row = y_lo * rows + p * (rows // 2)
+                    block = total[row : row + rows // 2, y_hi * 256 : (y_hi + 1) * 256]
+                    g[2 * wave + p][x, y_hi, y_lo] = block
 
 
 def proj_terms(ps, a01, a2, dy, mp, g):
@@ -200,7 +200,7 @@
                 row = y_lo * 96 + p * 48
                 total = (most[row : row + 48] + last[y_lo * 48 : y_lo * 48 + 48]).astype(BF16)
                 for y_hi in range(2):
-                    g[2 + p][x, y_hi, y_lo] = total[:, y_hi * 256 : (y_hi + 1) * 256]
+                    g[4 + p][x, y_hi, y_lo] = total[:, y_hi * 256 : (y_hi + 1) * 256]
 
 
 class Ring:
@@ -283,10 +283,10 @@
     dx_out, sums_out,
     x_v, dy_v, ws, ps, wt, pt,
     nxb, nxr, dxb, dxr, dab, dar, otb, otr,
-    qs, ks, vs, os, qt, kt, vt, ot, da, acc0, acc1, acc2,
+    qs, ks, vs, os, qt, kt, vt, ot, da, acc0, acc1, acc2, kept_s, kept_t,
     ht, at, hcat, a01, a2, dpk, dyf,
     spread_q, spread_p, mq, mp,
-    zs, zr,
+    zs1, zr1, zs2, zr2,
     send, recv, all_send, all_recv, local,
     *part_refs,
 ):
@@ -375,10 +375,12 @@
     def share_hidden(b):
         copies = []
         for i in range(2):
-            rows = pl.ds(pl.multiple_of((i * 2 + 1 - core) * QROWS, 32), QROWS)
-            copies.append(copy(ht.at[b, rows], hcat.at[b, pl.ds(i * QROWS, QROWS), far], pair))
-            rows = pl.ds(pl.multiple_of((i * 2 + core) * QROWS, 32), QROWS)
-            hcat[b, i * QROWS : (i + 1) * QROWS, :TOK] = ht[b, rows, :]
+            for first, rows in WAVES:
+                to = pl.ds(2 * first + i * rows, rows)
+                row = pl.multiple_of((i * 2 + 1 - core) * QROWS + first, 32)
+                copies.append(copy(ht.at[b, pl.ds(row, rows)], hcat.at[b, to, far], pair))
+                row = pl.multiple_of((i * 2 + core) * QROWS + first, 32)
+                hcat[b, to, :TOK] = ht[b, pl.ds(row, rows), :]
         return copies
 
     def share_attn(b):
@@ -410,17 +412,27 @@
         for c in copies:
             c.wait()
 
-    def last(b, found):
+    def last(b, found, zs, zr):
         total = jnp.concatenate([p.total() for p in found], axis=0).T
-        zs[b] = total.reshape(8, 32, ROWS).astype(BF16)
+        zs[b] = total.reshape(zs.shape[1:]).astype(BF16)
         return [copy(zs.at[b, lax.rem(z + k, 8)], zr.at[b, k], along_z(k)) for k in range(1, 8)]
 
-    def finish(b, copies):
+    def last_first(b, found):
+        return last(b, [found[0], found[1], found[4], found[5]], zs1, zr1)
+
+    def last_second(b, found):
+        return last(b, [found[2], found[3]], zs2, zr2)
+
+    def finish(b, copies, zs, zr, lanes):
         acc = zs[b, z].astype(F32)
         for k in range(1, 8):
             copies[k - 1].wait()
             acc = acc + zr[b, k].astype(F32)
-        sums_out[b] = acc
+        sums_out[b, :, lanes] = acc
+
+    def finish_both(b, first, second):
+        finish(b, first, zs1, zr1, slice(0, 256))
+        finish(b, second, zs2, zr2, slice(256, 384))
 
     SPACE, TIME = 0, 1
     space, time = parts(SPACE), parts(TIME)
@@ -433,18 +445,18 @@
     hidden = normed.astype(BF16)
     get_ws.wait()
     project(hidden, ws, (qs, ks, vs))
-    attention(qs, ks, vs, acc0, os, None)
+    attention(qs, ks, vs, acc0, os, kept_s, None)
     get_ps.wait()
     to_blocks((source + dot(os[:, :HD], ps[...])).astype(BF16), nxb)
+    pl.semaphore_wait(barrier, n + 2)
+    own_next = exchange_start(0, nxb, nxr)
     get_dy.wait()
     get_pt.wait()
-    dyf[TIME, :TOK, :] = dy_v[...]
     da[:, :HD] = dot(dy_v[...], pt[...], NT).astype(BF16)
     da[:, HD:] = jnp.zeros((TOK, PAD - HD), BF16)
     to_blocks(da[...], dab)
-    pl.semaphore_wait(barrier, n + 2)
-    own_next = exchange_start(0, nxb, nxr)
     own_da = exchange_start(1, dab, dar)
+    dyf[TIME, :TOK, :] = dy_v[...]
     ht[SPACE] = hidden.T
     at[SPACE] = os[...].T
     hidden_s = share_hidden(SPACE)
@@ -458,31 +470,35 @@
     hidden = normed.astype(BF16)
     project(hidden, wt, (qt, kt, vt))
     keep = same_position()
-    attention(qt, kt, vt, acc0, ot, keep)
+    attention(qt, kt, vt, acc0, ot, kept_t, keep)
     to_blocks(ot[...], otb)
     own_attn = exchange_start(3, otb, otr)
     ht[TIME] = hidden.T
     hidden_t = share_hidden(TIME)
     exchange_wait(1, dab, dar, own_da)
     da[...] = from_blocks(dar)
-    attention_back(qt, kt, vt, ot, da, accs, keep, {})
+    attention_back(qt, kt, vt, ot, da, accs, kept_t, {})
     pack(accs, dpk.at[TIME, own])
     hidden_t.append(share(dpk, TIME))
     middle = from_blocks(nxr).astype(F32)
     to_blocks(block_back(middle, wt, dpk.at[TIME, own]).astype(BF16), dxb)
     own_dx = exchange_start(2, dxb, dxr)
 
+    def both(found, p, step):
+        getattr(found[2 * p], step)()
+        getattr(found[2 * p + 1], step)()
+
     wait(hidden_t)
-    qkv_terms(spread_q, hcat.at[TIME], dpk.at[TIME], mq, [p.g for p in time])
-    time[0].first()
-    time[1].first()
+    qkv_spread(spread_q, dpk.at[TIME], mq)
+    for wave in range(2):
+        qkv_terms(wave, hcat.at[TIME], mq, [p.g for p in time])
+        both(time, wave, "first")
     exchange_wait(3, otb, otr, own_attn)
     at[TIME] = from_blocks(otr).T
     proj_t += share_attn(TIME)
     wait(proj_t)
     proj_terms(spread_p, a01.at[TIME], a2.at[TIME], dyf.at[TIME], mp, [p.g for p in time])
-    time[2].first()
-    time[3].first()
+    both(time, 2, "first")
 
     exchange_wait(2, dxb, dxr, own_dx)
     dy = (dy_v[...].astype(F32) + from_blocks(dxr).astype(F32)).astype(BF16)
@@ -491,53 +507,53 @@
     da[:, :HD] = dot(dy, ps[...], NT).astype(BF16)
     da[:, HD:] = jnp.zeros((TOK, PAD - HD), BF16)
 
-    def hook_a():
-        time[0].second()
-        time[1].second()
-
-    def hook_b():
+    def seconds_qkv():
+        both(time, 0, "second")
+        both(time, 1, "second")
+
+    def proj_set_out():
         wait(proj_s)
         proj_terms(spread_p, a01.at[SPACE], a2.at[SPACE], dyf.at[SPACE], mp, [p.g for p in space])
-        space[2].first()
-        space[3].first()
-
-    def hook_c():
-        time[2].second()
-        time[3].second()
-
-    hooks = {0: hook_a, 3: hook_b, 6: hook_c}
-    attention_back(qs, ks, vs, os, da, accs, None, hooks)
+        both(space, 2, "first")
+
+    def seconds_proj():
+        both(time, 2, "second")
+
+    hooks = {0: seconds_qkv, 5: seconds_proj}
+    attention_back(qs, ks, vs, os, da, accs, kept_s, hooks)
     pack(accs, dpk.at[SPACE, own])
     hidden_s.append(share(dpk, SPACE))
+    proj_set_out()
     for p in time:
         p.across()
     wait(hidden_s)
-    qkv_terms(spread_q, hcat.at[SPACE], dpk.at[SPACE], mq, [p.g for p in space])
-    space[0].first()
-    space[1].first()
-    space[2].second()
-    space[3].second()
-    along = last(TIME, time)
+    qkv_spread(spread_q, dpk.at[SPACE], mq)
+    for wave in range(2):
+        qkv_terms(wave, hcat.at[SPACE], mq, [p.g for p in space])
+        both(space, wave, "first")
+    both(space, 2, "second")
+    along_t = last_first(TIME, time), last_second(TIME, time)
+    both(space, 0, "second")
+    both(space, 1, "second")
+    both(space, 2, "across")
     dx_s = block_back(x_v[...].astype(F32), ws, dpk.at[SPACE, own])
     dx_out[...] = (dyf[SPACE, :TOK, :].astype(F32) + dx_s).astype(BF16)
-    space[0].second()
-    space[1].second()
-    space[2].across()
-    space[3].across()
-    finish(TIME, along)
-    space[0].across()
-    space[1].across()
-    finish(SPACE, last(SPACE, space))
+    both(space, 0, "across")
+    both(space, 1, "across")
+    finish_both(TIME, *along_t)
+    along_1 = last_first(SPACE, space)
+    finish_both(SPACE, along_1, last_second(SPACE, space))
 
 
 def outputs_kernel(dx, sums, dx_out, gqs, gps, gqt, gpt):
     dx_out[...] = dx[...]
     for b, (qkv, proj) in enumerate(((gqs, gps), (gqt, gpt))):
         block = sums[b]
-        qkv[...] = block[:27, :QROWS]
-        proj[:, 0:96] = block[:18, QROWS:]
-        proj[0:9, 96:144] = block[18:27, QROWS : QROWS + 48]
-        proj[9:18, 96:144] = block[18:27, QROWS + 48 :]
+        qkv[:, 0:160] = block[:27, 0:160]
+        qkv[:, 160:QROWS] = block[:27, 256:ROWS]
+        proj[:, 0:96] = block[:18, 160:256]
+        proj[0:9, 96:144] = block[18:27, 160:208]
+        proj[9:18, 96:144] = block[18:27, 208:256]
 
 
 def per_device(latents, out_grad, qkv_spatial, proj_spatial, qkv_temporal, proj_temporal):
@@ -569,19 +585,21 @@
             wide, wide, qkv, proj, qkv, proj,
             *[blocks] * 4, *[small] * 4,
             *[narrow] * 9, acc, acc, acc,
+            *[VMEM((HEADS, TOK, TOK), BF16)] * 2,
             VMEM((2, D, TOK), BF16),
             VMEM((2, PAD, TOK), BF16),
             VMEM((2, 2 * QROWS, 2 * TOK), BF16),
             VMEM((2, 192, 2 * TOK), BF16),
             VMEM((2, 96, 2 * TOK), BF16),
-            VMEM((2, 2 * TOK, 3 * PAD), BF16),
+            VMEM((2, 2 * TOK, WIDE), BF16),
             VMEM((2, 2 * TOK, D), BF16),
             VMEM((TILES, QWIN, 128), BF16),
             VMEM((TILES, PWIN, 384), BF16),
-            VMEM((2 * TOK, 512), BF16),
+            VMEM((2 * TOK, TILES * 128), BF16),
             VMEM((3, 2 * TOK, 512), BF16),
-            *[VMEM((2, 8, 32, ROWS), BF16)] * 2,
-            dma((102,)), dma((102,)), dma((4,)), dma((4,)), dma((10,)),
+            *[VMEM((2, 8, 32, 256), BF16)] * 2,
+            *[VMEM((2, 8, 32, 128), BF16)] * 2,
+            dma((156,)), dma((156,)), dma((4,)), dma((4,)), dma((10,)),
             *part_refs,
         ],
         name="both_blocks",

time: 108 us -> 101 us (0.935); the launches traced: 108 us -> 99.3 us
  Pallas kernels: 107 us -> 98.7 us
    pallas_call x1, Pallas kernels: 105 us -> 96.7 us  [per_device(): pl.pallas_call(kernel, out_shape=[jax.ShapeDtypeStruct((TOK, D), BF16), j...]
where the time goes in v3:
time: 101 us; the launch traced here: 99.3 us
  Pallas kernels  98.7 us (98%)
    pallas_call x1, Pallas kernels, per_device(): pl.pallas_call(kernel, out_shape=[jax.ShapeDtypeStruct((TOK, D), BF16), j...  96.7 us

profile of v3, /device:TPU:8, one launch (start us, length us, event | category | flops | bytes accessed | tf_op | source)
XLA Modules:
  0.0 99.3 jit_solution(2331769472047645139)
XLA Ops:
  0.6 96.7 %both_blocks.1 = (bf16[256,1152]{1,0:T(8,128)(2,1)}, f32[2,32,384]{2,1,0:T(8,128)}) custom-call(bf16[256,1152]{1,0:T(8,128)(2,1)} %bitcast.7, bf16[256,1152]{1,0:T(8,128)(2,1)} %bitcast.8, bf16[1728,1152]{1,0:T(8,128)(2,1)} %ws_in.1, bf16[576,1152]{1,0:T(8,128)(2,1)} %bitcast.5, bf16[1728,1152]{1,0:T(8,128)(2,1)} %wt_in.1, bf16[576,1152]{1,0:T(8,128)(2,1)} %bitcast.6), custom_call_target="tpu_custom_call" | custom-call | tf_op jit(solution)/shard_map/both_blocks/pallas_call | solution.py:576
  97.3 2.0 %outputs.1 = (bf16[256,1152]{1,0:T(8,128)(2,1)}, f32[27,288]{1,0:T(8,128)}, f32[18,144]{1,0:T(8,128)}, f32[27,288]{1,0:T(8,128)}, f32[18,144]{1,0:T(8,128)}) custom-call(bf16[256,1152]{1,0:T(8,128)(2,1)} %get-tuple-element.12.dx, f32[2,32,384]{2,1,0:T(8,128)} %get-tuple-element.13.sums), custom_call_target="tpu_custom_call" | custom-call | tf_op jit(solution)/shard_map/outputs/pallas_call | solution.py:612

commit v4 on v3

--- a/solution.py
+++ b/solution.py
@@ -25,8 +25,8 @@
 QROWS = 288
 PROWS = 96
 ROWS = QROWS + PROWS
-PARTS = ((80, True), (80, False), (64, True), (64, False), (48, True), (48, False))
-WAVES = ((0, 160), (160, 128))
+PARTS = ((64, True), (64, False), (80, True), (80, False), (48, True), (48, False))
+WAVES = ((0, 128), (128, 160))
 TILES = 16
 QWIN = 384
 PWIN = 256
@@ -165,11 +165,11 @@
         ps[tile, :, 256:384] = choice(low, PWIN, 18 * shard + 9, 18, 9, 36)
 
 
-def qkv_spread(qs, dpk, mq):
+def qkv_spread(qs, dpk, mq, rows):
     for tile in range(TILES):
         low = qlow(tile)
-        spread = dot(dpk[:, low : low + QWIN], qs[tile])
-        mq[:, tile * 128 : (tile + 1) * 128] = spread.astype(BF16)
+        spread = dot(dpk[rows, low : low + QWIN], qs[tile])
+        mq[rows, tile * 128 : (tile + 1) * 128] = spread.astype(BF16)
 
 
 def qkv_terms(wave, hcat, mq, g):
@@ -418,10 +418,10 @@
         return [copy(zs.at[b, lax.rem(z + k, 8)], zr.at[b, k], along_z(k)) for k in range(1, 8)]
 
     def last_first(b, found):
-        return last(b, [found[0], found[1], found[4], found[5]], zs1, zr1)
+        return last(b, found[:2], zs1, zr1)
 
     def last_second(b, found):
-        return last(b, [found[2], found[3]], zs2, zr2)
+        return last(b, found[2:], zs2, zr2)
 
     def finish(b, copies, zs, zr, lanes):
         acc = zs[b, z].astype(F32)
@@ -431,8 +431,8 @@
         sums_out[b, :, lanes] = acc
 
     def finish_both(b, first, second):
-        finish(b, first, zs1, zr1, slice(0, 256))
-        finish(b, second, zs2, zr2, slice(256, 384))
+        finish(b, first, zs1, zr1, slice(0, 128))
+        finish(b, second, zs2, zr2, slice(128, 384))
 
     SPACE, TIME = 0, 1
     space, time = parts(SPACE), parts(TIME)
@@ -489,7 +489,7 @@
         getattr(found[2 * p + 1], step)()
 
     wait(hidden_t)
-    qkv_spread(spread_q, dpk.at[TIME], mq)
+    qkv_spread(spread_q, dpk.at[TIME], mq, slice(0, 2 * TOK))
     for wave in range(2):
         qkv_terms(wave, hcat.at[TIME], mq, [p.g for p in time])
         both(time, wave, "first")
@@ -511,11 +511,6 @@
         both(time, 0, "second")
         both(time, 1, "second")
 
-    def proj_set_out():
-        wait(proj_s)
-        proj_terms(spread_p, a01.at[SPACE], a2.at[SPACE], dyf.at[SPACE], mp, [p.g for p in space])
-        both(space, 2, "first")
-
     def seconds_proj():
         both(time, 2, "second")
 
@@ -523,25 +518,28 @@
     attention_back(qs, ks, vs, os, da, accs, kept_s, hooks)
     pack(accs, dpk.at[SPACE, own])
     hidden_s.append(share(dpk, SPACE))
-    proj_set_out()
+    qkv_spread(spread_q, dpk.at[SPACE], mq, slice(0, TOK))
     for p in time:
         p.across()
     wait(hidden_s)
-    qkv_spread(spread_q, dpk.at[SPACE], mq)
+    qkv_spread(spread_q, dpk.at[SPACE], mq, slice(TOK, 2 * TOK))
     for wave in range(2):
         qkv_terms(wave, hcat.at[SPACE], mq, [p.g for p in space])
         both(space, wave, "first")
-    both(space, 2, "second")
+    wait(proj_s)
+    proj_terms(spread_p, a01.at[SPACE], a2.at[SPACE], dyf.at[SPACE], mp, [p.g for p in space])
+    both(space, 2, "first")
+    both(space, 0, "second")
     along_t = last_first(TIME, time), last_second(TIME, time)
-    both(space, 0, "second")
     both(space, 1, "second")
-    both(space, 2, "across")
     dx_s = block_back(x_v[...].astype(F32), ws, dpk.at[SPACE, own])
     dx_out[...] = (dyf[SPACE, :TOK, :].astype(F32) + dx_s).astype(BF16)
     both(space, 0, "across")
+    both(space, 2, "second")
     both(space, 1, "across")
+    along_1 = last_first(SPACE, space)
+    both(space, 2, "across")
     finish_both(TIME, *along_t)
-    along_1 = last_first(SPACE, space)
     finish_both(SPACE, along_1, last_second(SPACE, space))
 
 
@@ -549,11 +547,10 @@
     dx_out[...] = dx[...]
     for b, (qkv, proj) in enumerate(((gqs, gps), (gqt, gpt))):
         block = sums[b]
-        qkv[:, 0:160] = block[:27, 0:160]
-        qkv[:, 160:QROWS] = block[:27, 256:ROWS]
-        proj[:, 0:96] = block[:18, 160:256]
-        proj[0:9, 96:144] = block[18:27, 160:208]
-        proj[9:18, 96:144] = block[18:27, 208:256]
+        qkv[...] = block[:27, :QROWS]
+        proj[:, 0:96] = block[:18, QROWS:]
+        proj[0:9, 96:144] = block[18:27, QROWS : QROWS + 48]
+        proj[9:18, 96:144] = block[18:27, QROWS + 48 :]
 
 
 def per_device(latents, out_grad, qkv_spatial, proj_spatial, qkv_temporal, proj_temporal):
@@ -597,8 +594,8 @@
             VMEM((TILES, PWIN, 384), BF16),
             VMEM((2 * TOK, TILES * 128), BF16),
             VMEM((3, 2 * TOK, 512), BF16),
+            *[VMEM((2, 8, 32, 128), BF16)] * 2,
             *[VMEM((2, 8, 32, 256), BF16)] * 2,
-            *[VMEM((2, 8, 32, 128), BF16)] * 2,
             dma((156,)), dma((156,)), dma((4,)), dma((4,)), dma((10,)),
             *part_refs,
         ],

time: 101 us -> 100 us (0.990); the launches traced: 99.3 us -> 100 us
  no operation moved by 1% of the time
where the time goes in v4:
time: 100 us
  Pallas kernels  99.6 us (100%)
    pallas_call x1, Pallas kernels, per_device(): pl.pallas_call(kernel, out_shape=[jax.ShapeDtypeStruct((TOK, D), BF16), j...  97.6 us

profile of v4, /device:TPU:8, one launch (start us, length us, event | category | flops | bytes accessed | tf_op | source)
XLA Modules:
  0.0 100.2 jit_solution(17311146839960354470)
XLA Ops:
  0.6 97.6 %both_blocks.1 = (bf16[256,1152]{1,0:T(8,128)(2,1)}, f32[2,32,384]{2,1,0:T(8,128)}) custom-call(bf16[256,1152]{1,0:T(8,128)(2,1)} %bitcast.7, bf16[256,1152]{1,0:T(8,128)(2,1)} %bitcast.8, bf16[1728,1152]{1,0:T(8,128)(2,1)} %ws_in.1, bf16[576,1152]{1,0:T(8,128)(2,1)} %bitcast.5, bf16[1728,1152]{1,0:T(8,128)(2,1)} %wt_in.1, bf16[576,1152]{1,0:T(8,128)(2,1)} %bitcast.6), custom_call_target="tpu_custom_call" | custom-call | tf_op jit(solution)/shard_map/both_blocks/pallas_call | solution.py:573
  98.3 1.9 %outputs.1 = (bf16[256,1152]{1,0:T(8,128)(2,1)}, f32[27,288]{1,0:T(8,128)}, f32[18,144]{1,0:T(8,128)}, f32[27,288]{1,0:T(8,128)}, f32[18,144]{1,0:T(8,128)}) custom-call(bf16[256,1152]{1,0:T(8,128)(2,1)} %get-tuple-element.12.dx, f32[2,32,384]{2,1,0:T(8,128)} %get-tuple-element.13.sums), custom_call_target="tpu_custom_call" | custom-call | tf_op jit(solution)/shard_map/outputs/pallas_call | solution.py:609

commit v5 on v4

--- a/solution.py
+++ b/solution.py
@@ -532,15 +532,16 @@
     both(space, 0, "second")
     along_t = last_first(TIME, time), last_second(TIME, time)
     both(space, 1, "second")
-    dx_s = block_back(x_v[...].astype(F32), ws, dpk.at[SPACE, own])
-    dx_out[...] = (dyf[SPACE, :TOK, :].astype(F32) + dx_s).astype(BF16)
     both(space, 0, "across")
     both(space, 2, "second")
     both(space, 1, "across")
     along_1 = last_first(SPACE, space)
     both(space, 2, "across")
+    along_2 = last_second(SPACE, space)
+    dx_s = block_back(x_v[...].astype(F32), ws, dpk.at[SPACE, own])
+    dx_out[...] = (dyf[SPACE, :TOK, :].astype(F32) + dx_s).astype(BF16)
     finish_both(TIME, *along_t)
-    finish_both(SPACE, along_1, last_second(SPACE, space))
+    finish_both(SPACE, along_1, along_2)
 
 
 def outputs_kernel(dx, sums, dx_out, gqs, gps, gqt, gpt):

time: 100 us -> 100 us (level)
  no operation moved by 1% of the time
where the time goes in v5:
time: 100 us
  Pallas kernels  99.6 us (100%)
    pallas_call x1, Pallas kernels, per_device(): pl.pallas_call(kernel, out_shape=[jax.ShapeDtypeStruct((TOK, D), BF16), j...  97.6 us

profile of v5, /device:TPU:8, one launch (start us, length us, event | category | flops | bytes accessed | tf_op | source)
XLA Modules:
  0.0 100.2 jit_solution(13364138836533650826)
XLA Ops:
  0.6 97.6 %both_blocks.1 = (bf16[256,1152]{1,0:T(8,128)(2,1)}, f32[2,32,384]{2,1,0:T(8,128)}) custom-call(bf16[256,1152]{1,0:T(8,128)(2,1)} %bitcast.7, bf16[256,1152]{1,0:T(8,128)(2,1)} %bitcast.8, bf16[1728,1152]{1,0:T(8,128)(2,1)} %ws_in.1, bf16[576,1152]{1,0:T(8,128)(2,1)} %bitcast.5, bf16[1728,1152]{1,0:T(8,128)(2,1)} %wt_in.1, bf16[576,1152]{1,0:T(8,128)(2,1)} %bitcast.6), custom_call_target="tpu_custom_call" | custom-call | tf_op jit(solution)/shard_map/both_blocks/pallas_call | solution.py:574
  98.3 1.9 %outputs.1 = (bf16[256,1152]{1,0:T(8,128)(2,1)}, f32[27,288]{1,0:T(8,128)}, f32[18,144]{1,0:T(8,128)}, f32[27,288]{1,0:T(8,128)}, f32[18,144]{1,0:T(8,128)}) custom-call(bf16[256,1152]{1,0:T(8,128)(2,1)} %get-tuple-element.12.dx, f32[2,32,384]{2,1,0:T(8,128)} %get-tuple-element.13.sums), custom_call_target="tpu_custom_call" | custom-call | tf_op jit(solution)/shard_map/outputs/pallas_call | solution.py:610
